TPU v7x, 32 devices: a whole 2x2x4 slice. The times are simulated.
32 devices in a mesh: sib: 2 (over x), row: 4 (over y, core), col: 4 (over z).
Axes of the slice: x: 2, y: 2, z: 4, core: 2. Of those that a mesh axis runs over, the one named last changes fastest.
Arguments:
- child_tiles: float32 [2, 16, 32, 128, 128], P('sib', ('row', 'col')), may hold values from -6 to 6
- child_rows: int32 [2, 64], P('sib'), may hold values from 0 to 127, as said below
- child_slots: int32 [2, 16, 32], P('sib', ('row', 'col')), may hold values from 0 to 4095, as said below
- tile_count: int32 [2, 16], P('sib', ('row', 'col')), may hold values from 16 to 32, as said below
- inverses: float32 [2, 512, 512], replicated, as said below
Outputs:
- factored: float32 [16, 8, 32, 4, 128, 128], P(None, ('sib', 'row'), None, 'col')
Inputs may be any that keep to these rules, and one draw needn't show every extreme that they name: `child_rows`: A child's entries are distinct; entry i leaves the same remainder as i when divided by the number of grid rows of the parent. `child_slots`: call the owner of parent tile (I, J) the grid row I mod (number of grid rows) and grid column J mod (number of grid columns). Among the live slots of one device at most 2 carry tiles with one owner; in every draw some device reaches 2 for some owner. `tile_count`: some device of each child has all 32 slots live. `inverses`: each matrix is lower triangular with positive diagonal.
All inputs are finite; a program needn't handle non-finite values.
Results may differ from a plain program's by a relative error of at most 0.00012.
Values sent between devices are 32-bit elements; how exact they have to be, the bound alone decides.
A program may use at most 192 MiB of HBM per device.

v0:
```python
import jax
import jax.numpy as jnp
from jax import lax
from jax.sharding import PartitionSpec as P

NF = 16384
TILE = 128
PANEL = 512
NPANEL = 2
CHILD_TILES = 64
CAP = 2


def broadcast(value, axis, source):
    kept = jnp.where(lax.axis_index(axis) == source, value, 0).astype(value.dtype)
    return lax.psum(kept, axis)


def local(child_tiles, child_rows, child_slots, tile_count, inverses):
    grid_rows = lax.axis_size("sib") * lax.axis_size("row")
    columns = lax.axis_size("col")
    devices = grid_rows * columns
    tile_order = NF // TILE
    local_rows = tile_order // grid_rows
    local_cols = tile_order // columns
    tile_data = child_tiles[0, 0]
    slot_ids = child_slots[0, 0]
    live_count = tile_count[0, 0]
    row_list = child_rows[0]
    slot_total = slot_ids.shape[0]
    child_row = slot_ids // CHILD_TILES
    child_col = slot_ids % CHILD_TILES
    positions = jnp.arange(CHILD_TILES, dtype=jnp.int32)
    parent_row = jnp.sum(
        jnp.where(child_row[:, None] == positions[None, :], row_list[None, :], 0), axis=1
    )
    parent_col = jnp.sum(
        jnp.where(child_col[:, None] == positions[None, :], row_list[None, :], 0), axis=1
    )
    owner_index = parent_row % grid_rows * columns + parent_col % columns
    target = parent_row // grid_rows * local_cols + parent_col // columns
    slot_order = jnp.arange(slot_total, dtype=jnp.int32)
    is_live = slot_order < live_count
    earlier = (
        (owner_index[:, None] == owner_index[None, :])
        & is_live[None, :]
        & (slot_order[None, :] < slot_order[:, None])
    )
    slot_rank = jnp.sum(earlier.astype(jnp.int32), axis=1)
    slot_place = jnp.where(is_live, owner_index * CAP + slot_rank, devices * CAP)
    outgoing = (
        jnp.zeros((devices * CAP, TILE, TILE), jnp.float32)
        .at[slot_place]
        .set(tile_data, mode="drop")
    )
    destined = jnp.zeros((devices * CAP,), jnp.int32).at[slot_place].set(target, mode="drop")
    arrived, landing = (
        lax.all_to_all(
            outgoing.reshape(devices, CAP, TILE, TILE),
            ("sib", "row", "col"),
            split_axis=0,
            concat_axis=0,
            tiled=True,
        ),
        lax.all_to_all(
            destined.reshape(devices, CAP),
            ("sib", "row", "col"),
            split_axis=0,
            concat_axis=0,
            tiled=True,
        ),
    )
    front_tiles = jnp.zeros((local_rows * local_cols, TILE, TILE), jnp.float32)
    front_tiles = front_tiles.at[landing.reshape(-1)].add(arrived.reshape(-1, TILE, TILE))
    front_tiles = front_tiles.reshape(local_rows, local_cols, TILE, TILE)
    my_row = lax.axis_index(("sib", "row"))
    my_col = lax.axis_index("col")
    panel_tiles = PANEL // TILE
    root_count = grid_rows // columns
    tile_ids = jnp.arange(local_rows, dtype=jnp.int32) * grid_rows + my_row
    for panel_step in range(NPANEL):
        first_tile = panel_tiles * panel_step
        below_tile = first_tile + panel_tiles
        column_slot = first_tile // columns
        start_col = first_tile % columns
        is_below = tile_ids >= below_tile
        weights = inverses[panel_step]
        column_block = front_tiles[:, column_slot]
        holds_panel = (my_col >= start_col) & (my_col < start_col + panel_tiles)
        offset = jnp.clip(my_col - start_col, 0, panel_tiles - 1)
        everyone = lax.all_gather(column_block[None], "col", axis=0, tiled=True)
        chosen = everyone[start_col : start_col + panel_tiles]
        panel_rows = chosen.transpose(1, 2, 0, 3).reshape(local_rows * TILE, PANEL)
        factor = jnp.dot(panel_rows, weights.T, precision=lax.Precision.HIGHEST)
        factor = (
            factor.reshape(local_rows, TILE, PANEL) * is_below.astype(jnp.float32)[:, None, None]
        )
        panel_piece = lax.dynamic_slice_in_dim(factor, offset * TILE, TILE, 2)
        replace = is_below[:, None, None] & holds_panel
        front_tiles = front_tiles.at[:, column_slot].set(
            jnp.where(replace, panel_piece, column_block)
        )
        received = [
            broadcast(factor, ("sib", "row"), root_step * columns + my_col)
            for root_step in range(root_count)
        ]
        column_factor = jnp.stack(received, 1).reshape(local_cols, TILE, PANEL)
        front_tiles = front_tiles - jnp.einsum(
            "aip,bjp->abij", factor, column_factor, precision=lax.Precision.HIGHEST
        )
    return front_tiles.reshape(local_rows, 1, local_cols, 1, TILE, TILE)


def solution(mesh):
    return jax.shard_map(
        local,
        mesh=mesh,
        in_specs=(
            P("sib", ("row", "col"), None, None, None),
            P("sib", None),
            P("sib", ("row", "col"), None),
            P("sib", ("row", "col")),
            P(),
        ),
        out_specs=P(None, ("sib", "row"), None, "col", None, None),
        check_vma=False,
    )
```

profile of v0, /device:TPU:2, one launch (start us, length us, event | category | flops | bytes accessed | tf_op | source)
XLA Modules:
  0.0 780.0 jit_solution(6619373930247690881)
XLA Ops:
  7.4 0.7 and_select_fusion.7
  8.0 0.8 select_reduce_fusion
  8.9 0.2 convert_reduce_fusion
  9.1 0.7 scatter_custom_fusion
  9.8 0.7 all_to_all.9
  10.5 6.1 all-to-all-start
  16.6 2.5 broadcast_in_dim.66
  19.1 5.5 scatter_fusion
  24.7 5.7 all-to-all-start.1
  30.4 0.0 all-gather.5.cloned.1.call-start
  30.4 0.5 broadcast.441
  31.0 0.6 reduce.7
  31.6 0.1 reshape.347
  31.7 89.0 %all-to-all-done.1 = f32[32,2,128,128]{3,2,1,0:T(8,128)} async-done(((f32[32,2,128,128]{3,2,1,0:T(8,128)}), f32[32,2,128,128]{3,2,1,0:T(8,128)}, u32[]{:S(2)}, u32[]{:S(2)}) %all-to-all-start.1) | async-done | bytes 4194336 | tf_op jit(solution)/shard_map/all_to_all | solution.py:58
  120.7 11.5 %broadcast_in_dim.62 = f32[512,128,128]{2,1,0:T(8,128)} broadcast(f32[]{:T(128)} %constant.138.clone.1), dimensions={} | broadcast | bytes 33554436 | tf_op jit(solution)/shard_map/broadcast_in_dim | solution.py:73
  132.1 13.9 %scatter_fusion.1 = f32[512,128,128]{2,1,0:T(8,128)} fusion(f32[512,128,128]{2,1,0:T(8,128)} %broadcast_in_dim.62, s32[64]{0:T(128)S(1)} %fusion.14, f32[64,128,128]{2,1,0:T(8,128)} %bitcast.11), kind=kCustom, calls=%fused_computation.2 | custom fusion | flops 1048576 | bytes 12583168 | tf_op jit(solution)/shard_map/scatter-add | solution.py:74
  146.0 2.4 slice_bitcast_fusion.1
  148.5 0.0 all-reduce.7.cloned.1.call-start
  148.5 82.8 %all-gather.5.cloned.1.call-done = f32[64,1,128,128]{3,2,1,0:T(8,128)} async-done(((f32[16,1,128,128]{3,2,1,0:T(8,128)}), f32[64,1,128,128]{3,2,1,0:T(8,128)}) %all-gather.5.cloned.1.call-update) | async-done | bytes 4194320 | tf_op jit(solution)/shard_map/all_gather | solution.py:91
  231.3 6.9 copy.53
  238.3 5.6 dot_general.16
  243.9 8.6 %convolution_multiply_fusion.1 = f32[16,128,512]{2,1,0:T(8,128)S(1)} fusion(f32[16,128,512]{2,1,0:T(8,128)} %dot_general.16, f32[16]{0:T(128)S(1)} %get-tuple-element.49, f32[2,512,512]{2,1,0:T(8,128)S(1)} %copy-done.5), kind=kOutput, calls=%fused_computation.17 | convolution fusion | flops 6443499520 | bytes 9437696 | tf_op jit(solution)/shard_map/dot_general | solution.py:94
  252.6 4.7 select_bitcast_fusion.3
  257.2 0.0 all-reduce.7.cloned.1.call-update
  257.2 0.2 all-gather.7.cloned.1.call-start
  257.5 23.4 %copy.36 = f32[16,32,128,128]{3,2,0,1:T(8,128)} copy(f32[16,32,128,128]{3,2,1,0:T(8,128)} %bitcast.117) | data formatting | bytes 67108864 | tf_op jit(solution)/shard_map/reshape | solution.py:75
  280.9 2.4 bitcast_dynamic-update-slice_fusion.1
  283.2 99.5 %all-reduce.7.cloned.1.call-done = (f32[16,1,128,512]{3,2,0,1:T(8,128)}, f32[16,1,128,512]{3,2,0,1:T(8,128)}) async-done(((f32[16,1,128,512]{3,2,0,1:T(8,128)}, f32[16,1,128,512]{3,2,0,1:T(8,128)}), (f32[16,1,128,512]{3,2,0,1:T(8,128)}, f32[16,1,128,512]{3,2,0,1:T(8,128)})) %all-reduce.7.cloned.1.call-update) | async-done | bytes 8388624 | tf_op jit(solution)/shard_map/psum | solution.py:16
  382.7 4.5 pad_maximum_fusion
  387.2 1.6 copy.37
  388.7 0.6 copy-done.1
  389.3 59.3 %bitcast_subtract_fusion.1 = f32[16,32,128,128]{3,2,0,1:T(8,128)} fusion(f32[16,32,128,128]{3,2,0,1:T(8,128)} %bitcast_dynamic-update-slice_fusion.1, f32[32,128,512,1]{2,1,3,0:T(8,128)S(1)} %bitcast.118, f32[16,128,512]{2,1,0:T(8,128)S(1)} %copy-done.1), kind=kOutput, calls=%fused_computation.5 | convolution fusion | flops 51547996160 | bytes 79691776 | tf_op jit(solution)/shard_map/aip,bjp->abij/dot_general | solution.py:108
  448.7 2.4 slice_bitcast_fusion
  451.1 0.0 all-gather.7.cloned.1.call-update
  451.1 0.3 all-reduce.5.cloned.1.call-start
  451.4 81.0 %all-gather.7.cloned.1.call-done = f32[64,1,128,128]{3,2,1,0:T(8,128)} async-done(((f32[16,1,128,128]{3,2,1,0:T(8,128)}), f32[64,1,128,128]{3,2,1,0:T(8,128)}) %all-gather.7.cloned.1.call-update) | async-done | bytes 4194320 | tf_op jit(solution)/shard_map/all_gather | solution.py:91
  532.4 6.9 copy.52
  539.3 5.6 dot_general.19
  545.0 8.6 %convolution_multiply_fusion = f32[16,128,512]{2,1,0:T(8,128)S(1)} fusion(f32[16,128,512]{2,1,0:T(8,128)} %dot_general.19, f32[16]{0:T(128)S(1)} %get-tuple-element.47, f32[2,512,512]{2,1,0:T(8,128)S(1)} %copy-done.6), kind=kOutput, calls=%fused_computation.16 | convolution fusion | flops 6443499520 | bytes 9437696 | tf_op jit(solution)/shard_map/dot_general | solution.py:94
  553.6 4.5 select_bitcast_fusion.1
  558.2 0.0 all-reduce.5.cloned.1.call-update
  558.2 2.4 bitcast_dynamic-update-slice_fusion
  560.6 123.1 %all-reduce.5.cloned.1.call-done = (f32[16,1,128,512]{3,2,0,1:T(8,128)}, f32[16,1,128,512]{3,2,0,1:T(8,128)}) async-done(((f32[16,1,128,512]{3,2,0,1:T(8,128)}, f32[16,1,128,512]{3,2,0,1:T(8,128)}), (f32[16,1,128,512]{3,2,0,1:T(8,128)}, f32[16,1,128,512]{3,2,0,1:T(8,128)})) %all-reduce.5.cloned.1.call-update) | async-done | bytes 8388624 | tf_op jit(solution)/shard_map/psum | solution.py:16
  683.6 4.5 pad_maximum_fusion.1
  688.1 1.6 copy.41
  689.7 0.6 copy-done.3
  690.3 59.5 %fusion = f32[16,1,32,1,128,128]{5,4,0,2,3,1:T(8,128)} fusion(f32[16,32,128,128]{3,2,0,1:T(8,128)} %bitcast_dynamic-update-slice_fusion, f32[32,128,512,1]{2,1,3,0:T(8,128)S(1)} %bitcast.119, f32[16,128,512]{2,1,0:T(8,128)S(1)} %copy-done.3), kind=kOutput, calls=%fused_computation.4 | convolution fusion | flops 51547996160 | bytes 79691776 | tf_op jit(solution)/shard_map/aip,bjp->abij/dot_general | solution.py:108
  749.8 23.2 %copy.43 = f32[16,1,32,1,128,128]{5,4,3,2,1,0:T(8,128)} copy(f32[16,1,32,1,128,128]{5,4,0,2,3,1:T(8,128)} %fusion) | data formatting | bytes 67108864 | tf_op jit(solution)/shard_map/reshape | solution.py:111
  (20 shorter events, 0.1 us)
Async XLA Ops:
  6.5 12.6 %copy-start.4 = (f32[1,1,32,128,128]{4,3,2,1,0:T(8,128)S(1)}, f32[1,1,32,128,128]{4,3,2,1,0:T(8,128)}, u32[]{:S(2)}) copy-start(f32[1,1,32,128,128]{4,3,2,1,0:T(8,128)} %param.9) | copy-start | bytes 6291460
  10.5 14.2 %all-to-all-start = ((s32[32,1,2]{2,1,0:T(1,128)}), s32[32,1,2]{2,1,0:T(1,128)S(1)}, u32[]{:S(2)}, u32[]{:S(2)}) async-start(s32[32,1,2]{2,1,0:T(1,128)} %bitcast.7), calls=%async_computation | async-start | bytes 32768 | tf_op jit(solution)/shard_map/all_to_all | solution.py:65
  24.7 96.0 %all-to-all-start.1 = ((f32[32,2,128,128]{3,2,1,0:T(8,128)}), f32[32,2,128,128]{3,2,1,0:T(8,128)}, u32[]{:S(2)}, u32[]{:S(2)}) async-start(f32[32,2,128,128]{3,2,1,0:T(8,128)} %bitcast.120), calls=%async_computation.1 | async-start | bytes 8388608 | tf_op jit(solution)/shard_map/all_to_all | solution.py:58
  30.4 200.9 %all-gather.5.cloned.1.call-start = ((), (), s32[]{:S(2)}) async-start(), calls=%async_computation.2 | async-start | bytes 5242880 | tf_op jit(solution)/shard_map/all_gather | solution.py:91
  148.5 234.2 %all-reduce.7.cloned.1.call-start = ((), (), s32[]{:S(2)}) async-start(), calls=%async_computation.5 | async-start | bytes 16777216 | tf_op jit(solution)/shard_map/psum | solution.py:16
  238.3 5.6 copy-start.5
  252.6 4.7 copy-start
  257.2 275.2 %all-gather.7.cloned.1.call-start = ((), (), s32[]{:S(2)}) async-start(), calls=%async_computation.3 | async-start | bytes 5242880 | tf_op jit(solution)/shard_map/all_gather | solution.py:91
  387.2 2.2 copy-start.1
  451.1 232.5 %all-reduce.5.cloned.1.call-start = ((), (), s32[]{:S(2)}) async-start(), calls=%async_computation.4 | async-start | bytes 16777216 | tf_op jit(solution)/shard_map/psum | solution.py:16
  539.3 5.6 copy-start.6
  553.6 4.5 copy-start.2
  688.1 2.2 copy-start.3
Sparse Core Ops, SparseCore 0:
  148.6 82.7 all-gather.4
  257.4 125.2 all-reduce.6
  451.3 81.0 all-gather.6
  558.3 125.2 all-reduce.4
where the time goes:
time: 790 us; the launch traced here: 780 us
  waiting for transfers between devices  475 us (60%)
  matrix products  136 us (17%)
  local copies, waits for them, and re-layouts  103 us (13%)
  other arithmetic  39.1 us (5%)
  between operations  14.6 us (2%)
  starting transfers between devices  12.4 us (2%)
    psum x2, waiting for transfers between devices, broadcast(): return lax.psum(kept, axis)  223 us
    all_gather x2, waiting for transfers between devices, local(): everyone = lax.all_gather(column_block[None], 'col', axis=0, tiled=True)  164 us
    dot_general x2, matrix products, local(): jnp.einsum('aip,bjp->abij', factor, column_factor, precision=lax.Precisio...  119 us
    all_to_all x1, waiting for transfers between devices, local(): lax.all_to_all(outgoing.reshape(devices, CAP, TILE, TILE), ('sib', 'row',...  89 us
    reshape x1, local copies, waits for them, and re-layouts, local(): front_tiles = front_tiles.reshape(local_rows, local_cols, TILE, TILE)  23.4 us
    reshape x1, local copies, waits for them, and re-layouts, local(): return front_tiles.reshape(local_rows, 1, local_cols, 1, TILE, TILE)  23.2 us
    another operation x4, other arithmetic, local(): column_factor = jnp.stack(received, 1).reshape(local_cols, TILE, PANEL)  18.1 us
    dot_general x2, matrix products, local(): factor = jnp.dot(panel_rows, weights.T, precision=lax.Precision.HIGHEST)  17.3 us
  transfers between devices with their start and end apart: 6, of which 5 were waited for; matrix products, arithmetic and copies ran while one was open for 5% of the time, Pallas kernels for 0%

commit v1 on v0

--- a/solution.py
+++ b/solution.py
@@ -1,6 +1,10 @@
+import functools
+
 import jax
 import jax.numpy as jnp
 from jax import lax
+from jax.experimental import pallas as pl
+from jax.experimental.pallas import tpu as pltpu
 from jax.sharding import PartitionSpec as P
 
 NF = 16384
@@ -111,9 +115,457 @@
     return front_tiles.reshape(local_rows, 1, local_cols, 1, TILE, TILE)
 
 
+def route(child_rows, child_slots, tile_count, grid_rows, columns, local_cols):
+    slot_ids = child_slots[0, 0]
+    row_list = child_rows[0]
+    slot_total = slot_ids.shape[0]
+    positions = jnp.arange(CHILD_TILES, dtype=jnp.int32)
+
+    def look_up(index):
+        return jnp.sum(jnp.where(index[:, None] == positions[None, :], row_list[None, :], 0), axis=1)
+
+    parent_row = look_up(slot_ids // CHILD_TILES)
+    parent_col = look_up(slot_ids % CHILD_TILES)
+    owner_index = parent_row % grid_rows * columns + parent_col % columns
+    target = parent_row // grid_rows * local_cols + parent_col // columns
+    slot_order = jnp.arange(slot_total, dtype=jnp.int32)
+    is_live = slot_order < tile_count[0, 0]
+    earlier = (
+        (owner_index[:, None] == owner_index[None, :])
+        & is_live[None, :]
+        & (slot_order[None, :] < slot_order[:, None])
+    )
+    slot_rank = jnp.sum(earlier.astype(jnp.int32), axis=1)
+    slot_place = jnp.where(is_live, owner_index * CAP + slot_rank, grid_rows * columns * CAP)
+    return slot_place, target
+
+
+def collect_kernel(local_cols, land_ref, tiles_ref, out_ref):
+    out_ref[...] = jnp.zeros_like(out_ref)
+
+    def step(n, carry):
+        place = land_ref[n] - 1
+        b = lax.rem(place, local_cols)
+
+        @pl.when((place >= 0) & (b < NPANEL))
+        def _():
+            a = place // local_cols
+            out_ref[b, a] = out_ref[b, a] + tiles_ref[n]
+
+        return carry
+
+    lax.fori_loop(0, land_ref.shape[0], step, 0)
+
+
+def exchange_kernel(
+    p_ref, s_ref, z_ref,
+    own_sem, g_recv, up_send, down_send,
+    h_recv, x_send, y_send, core_send, copy_sem,
+    z_local, z_send, z_recv,
+):
+    x = lax.axis_index("sib")
+    r = lax.axis_index("row")
+    z = lax.axis_index("col")
+    last = lax.axis_size("col") - 1
+    y, core = r // 2, lax.rem(r, 2)
+    right_core = core == lax.rem(z, 2)
+    is_source = right_core & (y == z // 2)
+    is_relay = right_core & (y != z // 2)
+    up, down = (x, r, z + 1), (x, r, z - 1)
+    x_peer = (1 - x, r, z)
+    y_peer = (x, lax.rem(r + 2, 4), z)
+    core_peer = (x, r + 1 - 2 * core, z)
+    has_up, has_down = z < last, z > 0
+
+    def remote(src, dst, send, recv, device):
+        return pltpu.make_async_remote_copy(
+            src_ref=src, dst_ref=dst, send_sem=send, recv_sem=recv,
+            device_id=device, device_id_type=pl.DeviceIdType.MESH,
+        )
+
+    barrier = pltpu.get_barrier_semaphore()
+    for peer in (x_peer, y_peer, core_peer):
+        pl.semaphore_signal(barrier, inc=1, device_id=peer, device_id_type=pl.DeviceIdType.MESH)
+
+    @pl.when(has_up)
+    def _():
+        pl.semaphore_signal(barrier, inc=1, device_id=up, device_id_type=pl.DeviceIdType.MESH)
+
+    @pl.when(has_down)
+    def _():
+        pl.semaphore_signal(barrier, inc=1, device_id=down, device_id_type=pl.DeviceIdType.MESH)
+
+    pl.semaphore_wait(barrier, 3 + jnp.where(has_up, 1, 0) + jnp.where(has_down, 1, 0))
+
+    def up_copy(src, c, p):
+        return remote(src, s_ref.at[0, c, p], up_send.at[c, p], g_recv.at[c, p], up)
+
+    def down_copy(src, c, p):
+        return remote(src, s_ref.at[0, c, p], down_send.at[c, p], g_recv.at[c, p], down)
+
+    def own_copy(p):
+        return pltpu.make_async_copy(p_ref.at[p], s_ref.at[0, z, p], own_sem.at[p])
+
+    def plane_copies(src, c, p):
+        there = s_ref.at[1 + x, c, p]
+        recv = h_recv.at[x, c, p]
+        return (
+            remote(src, there, x_send.at[c, p], recv, x_peer),
+            remote(src, there, y_send.at[c, p], recv, y_peer),
+            remote(src, there, core_send.at[x, c, p], recv, core_peer),
+            pltpu.make_async_copy(src, there, copy_sem.at[c, p]),
+        )
+
+    def relay_x(c, p):
+        here = s_ref.at[1 + x, c, p]
+        return remote(here, here, x_send.at[c, p], h_recv.at[x, c, p], x_peer)
+
+    def to_core(k, c, p):
+        here = s_ref.at[1 + k, c, p]
+        return remote(here, here, core_send.at[k, c, p], h_recv.at[k, c, p], core_peer)
+
+    def units(t):
+        if t == 0:
+            return [(z, None, 0)]
+        return [(z - t, z >= t, -1), (z + t, z + t <= last, 1)]
+
+    def guarded(condition, body):
+        if condition is None:
+            body()
+        else:
+            pl.when(condition)(body)
+
+    def gather_step(p, t):
+        for c, exists, side in units(t):
+            def body(c=c, side=side):
+                if side == 0:
+                    src = p_ref.at[p]
+                    own_copy(p).start()
+                else:
+                    src = s_ref.at[0, c, p]
+                    up_copy(src, c, p).wait_recv()
+                if side <= 0:
+                    pl.when(has_up)(lambda: up_copy(src, c, p).start())
+                if side >= 0:
+                    pl.when(has_down)(lambda: down_copy(src, c, p).start())
+
+                @pl.when(is_source)
+                def _():
+                    for copy in plane_copies(src, c, p):
+                        copy.start()
+
+            guarded(exists, body)
+
+    def relay_step(p, t):
+        for c, exists, side in units(t):
+            def body(c=c):
+                @pl.when(is_relay)
+                def _():
+                    to_core(x, c, p).wait_recv()
+                    relay_x(c, p).start()
+                    to_core(x, c, p).start()
+
+                @pl.when(right_core)
+                def _():
+                    to_core(1 - x, c, p).wait_recv()
+                    to_core(1 - x, c, p).start()
+
+            guarded(exists, body)
+
+    def corner_local():
+        return pltpu.make_async_copy(s_ref.at[0, :, 0, 0], z_ref.at[r], z_local)
+
+    def corner_x():
+        return remote(s_ref.at[0, :, 0, 0], z_ref.at[r], z_send.at[0], z_recv.at[0], x_peer)
+
+    def corner_core():
+        return remote(z_ref.at[r], z_ref.at[r], z_send.at[1], z_recv.at[1], core_peer)
+
+    def corner_y():
+        pair = z_ref.at[pl.ds(2 * y, 2)]
+        return remote(pair, pair, z_send.at[2], z_recv.at[2], y_peer)
+
+    steps = [(p, t) for p in range(NPANEL) for t in range(4)]
+    for n, (p, t) in enumerate(steps):
+        gather_step(p, t)
+        if n:
+            relay_step(*steps[n - 1])
+        if n == 4:
+            own_copy(0).wait()
+
+            @pl.when(x == 1)
+            def _():
+                corner_local().start()
+                corner_x().start()
+        if n == 5:
+            @pl.when(x == 1)
+            def _():
+                corner_local().wait()
+
+            @pl.when(x == 0)
+            def _():
+                corner_x().wait_recv()
+
+            corner_core().start()
+        if n == 6:
+            corner_core().wait_recv()
+            corner_y().start()
+    relay_step(*steps[-1])
+
+    own_copy(1).wait()
+    corner_y().wait_recv()
+    pl.when(x == 1)(lambda: corner_x().wait_send())
+    corner_core().wait_send()
+    corner_y().wait_send()
+    for p, t in steps:
+        for c, exists, side in units(t):
+            def body(c=c, side=side, p=p):
+                src = p_ref.at[p] if side == 0 else s_ref.at[0, c, p]
+                if side <= 0:
+                    pl.when(has_up)(lambda: up_copy(src, c, p).wait_send())
+                if side >= 0:
+                    pl.when(has_down)(lambda: down_copy(src, c, p).wait_send())
+
+                @pl.when(is_source)
+                def _():
+                    first, second, third, here = plane_copies(src, c, p)
+                    first.wait_send()
+                    second.wait_send()
+                    third.wait_send()
+                    here.wait()
+
+                @pl.when(is_relay)
+                def _():
+                    relay_x(c, p).wait_send()
+                    to_core(x, c, p).wait_send()
+
+                @pl.when(right_core)
+                def _():
+                    to_core(1 - x, c, p).wait_send()
+
+                @pl.when(jnp.logical_not(right_core))
+                def _():
+                    to_core(x, c, p).wait_recv()
+                    to_core(1 - x, c, p).wait_recv()
+
+            guarded(exists, body)
+
+
+def split(value):
+    high = value.astype(jnp.bfloat16)
+    return high, (value - high.astype(jnp.float32)).astype(jnp.bfloat16)
+
+
+def dot3(left, right):
+    dims = (((1,), (1,)), ((), ()))
+    dot = functools.partial(lax.dot_general, dimension_numbers=dims, preferred_element_type=jnp.float32)
+    return dot(left[0], right[0]) + (dot(left[0], right[1]) + dot(left[1], right[0]))
+
+
+def solve_kernel(where_ref, s_ref, z_ref, w_ref, high_ref, low_ref, own_ref, wh, wl, qh, ql, full):
+    slab, part = pl.program_id(0), pl.program_id(1)
+    rows = s_ref.shape[3]
+
+    @pl.when((slab == 0) & (part == 0))
+    def _():
+        for p in range(NPANEL):
+            wh[p], wl[p] = split(w_ref[p])
+        corner = jnp.concatenate([z_ref[:, c].reshape(PANEL, TILE) for c in range(4)], axis=1)
+        qh[...], ql[...] = split(dot3(split(corner), (wh[0], wl[0])))
+
+    def columns(p):
+        return jnp.concatenate(
+            [s_ref[0, c, p].reshape(rows * TILE, TILE) for c in range(4)], axis=1
+        )
+
+    a = part * rows + lax.broadcasted_iota(jnp.int32, (rows * TILE, 1), 0) // TILE
+    tile_row = a * 8 + where_ref[slab]
+    first = dot3(split(columns(0)), (wh[0], wl[0]))
+    first_parts = split(first)
+    rest = columns(1) - dot3(first_parts, (qh[...], ql[...]))
+    second = dot3(split(rest), (wh[1], wl[1]))
+    first = jnp.where(tile_row >= 4, first, 0.0)
+    second = jnp.where(tile_row >= 8, second, 0.0)
+    full[:, :PANEL] = first
+    full[:, PANEL:] = second
+    high, low = split(full[...])
+    high_ref[...] = high.reshape(high_ref.shape)
+    low_ref[...] = low.reshape(low_ref.shape)
+
+    @pl.when(slab == 0)
+    def _():
+        for p in range(NPANEL):
+            start = pl.multiple_of(p * PANEL + where_ref[3] * TILE, TILE)
+            own_ref[p] = full[:, pl.ds(start, TILE)].reshape(rows, TILE, TILE)
+
+
+def update_kernel(local_cols, where_ref, land_ref, rh_ref, rl_ref, ch_ref, cl_ref, tiles_ref, own_ref, out_ref):
+    step = pl.program_id(0)
+    a_total, b_block = out_ref.shape[0], out_ref.shape[1]
+    pairs = b_block // 2
+    a_block = 4
+    depth = rh_ref.shape[-1]
+
+    def chunk(i, carry):
+        a0 = i * a_block
+        left = tuple(ref[0, pl.ds(a0, a_block)].reshape(a_block * TILE, depth) for ref in (rh_ref, rl_ref))
+        for k in range(2):
+            right = tuple(ref[k].reshape(pairs * TILE, depth) for ref in (ch_ref, cl_ref))
+            product = -dot3(left, right)
+            for m in range(pairs):
+                out_ref[pl.ds(a0, a_block), 2 * m + k] = product[:, m * TILE : (m + 1) * TILE].reshape(
+                    a_block, TILE, TILE
+                )
+        return carry
+
+    lax.fori_loop(0, a_total // a_block, chunk, 0)
+
+    def add(n, carry):
+        place = land_ref[n] - 1
+        b = lax.rem(place, local_cols) - step * b_block
+
+        @pl.when((place >= 0) & (b >= 0) & (b < b_block))
+        def _():
+            a = place // local_cols
+            out_ref[a, b] = out_ref[a, b] + tiles_ref[n]
+
+        return carry
+
+    lax.fori_loop(0, land_ref.shape[0], add, 0)
+
+    @pl.when(step == 0)
+    def _():
+        for p in range(NPANEL):
+            @pl.when(where_ref[0] >= (p + 1) * 4)
+            def _():
+                out_ref[0, p] = own_ref[p, 0]
+
+            out_ref[1:, p] = own_ref[p, 1:]
+
+
+def local_fast(child_tiles, child_rows, child_slots, tile_count, inverses):
+    grid_rows = lax.axis_size("sib") * lax.axis_size("row")
+    columns = lax.axis_size("col")
+    devices = grid_rows * columns
+    tile_order = NF // TILE
+    local_rows = tile_order // grid_rows
+    local_cols = tile_order // columns
+    axes = ("sib", "row", "col")
+    slot_place, target = route(child_rows, child_slots, tile_count, grid_rows, columns, local_cols)
+    outgoing = (
+        jnp.zeros((devices * CAP, TILE, TILE), jnp.float32)
+        .at[slot_place]
+        .set(child_tiles[0, 0], mode="drop")
+    )
+    destined = jnp.zeros((devices * CAP,), jnp.int32).at[slot_place].set(target + 1, mode="drop")
+    arrived = lax.all_to_all(
+        outgoing.reshape(devices, CAP, TILE, TILE), axes, split_axis=0, concat_axis=0, tiled=True
+    ).reshape(devices * CAP, TILE, TILE)
+    landing = lax.all_to_all(
+        destined.reshape(devices, CAP), axes, split_axis=0, concat_axis=0, tiled=True
+    ).reshape(devices * CAP)
+
+    vmem = pl.BlockSpec(memory_space=pltpu.VMEM)
+    smem = pl.BlockSpec(memory_space=pltpu.SMEM)
+    anywhere = pl.BlockSpec(memory_space=pl.ANY)
+    panels = pl.pallas_call(
+        functools.partial(collect_kernel, local_cols),
+        out_shape=jax.ShapeDtypeStruct((NPANEL, local_rows, TILE, TILE), jnp.float32),
+        in_specs=[smem, vmem],
+        out_specs=vmem,
+        compiler_params=pltpu.CompilerParams(vmem_limit_bytes=24 * 2**20),
+        name="collect",
+    )(landing, arrived)
+
+    dma = pltpu.SemaphoreType.DMA
+    unit = (columns, NPANEL)
+    slabs, corner = pl.pallas_call(
+        exchange_kernel,
+        out_shape=(
+            jax.ShapeDtypeStruct((3, columns, NPANEL, local_rows, TILE, TILE), jnp.float32),
+            jax.ShapeDtypeStruct((4, columns, TILE, TILE), jnp.float32),
+        ),
+        in_specs=[anywhere],
+        out_specs=(anywhere, anywhere),
+        scratch_shapes=[
+            dma((NPANEL,)), dma(unit), dma(unit), dma(unit),
+            dma((2,) + unit), dma(unit), dma(unit), dma((2,) + unit), dma(unit),
+            dma, dma((3,)), dma((3,)),
+        ],
+        compiler_params=pltpu.CompilerParams(collective_id=0, has_side_effects=True),
+        name="exchange",
+    )(panels)
+
+    my_row = lax.axis_index(("sib", "row"))
+    my_col = lax.axis_index("col")
+    where = jnp.stack([my_row, my_col, my_col + 4, my_col]).astype(jnp.int32)
+    rows = 4
+    order = NPANEL * PANEL
+    factor_shape = jax.ShapeDtypeStruct((3, local_rows, TILE, order), jnp.bfloat16)
+    factor_spec = pl.BlockSpec((1, rows, TILE, order), lambda s, i, w: (s, i, 0, 0))
+    parts = local_rows // rows
+    high, low, own = pl.pallas_call(
+        solve_kernel,
+        grid_spec=pltpu.PrefetchScalarGridSpec(
+            num_scalar_prefetch=1,
+            grid=(3, parts),
+            in_specs=[
+                pl.BlockSpec((1, columns, NPANEL, rows, TILE, TILE), lambda s, i, w: (s, 0, 0, i, 0, 0)),
+                pl.BlockSpec((4, columns, TILE, TILE), lambda s, i, w: (0, 0, 0, 0)),
+                pl.BlockSpec((NPANEL, PANEL, PANEL), lambda s, i, w: (0, 0, 0)),
+            ],
+            out_specs=(
+                factor_spec,
+                factor_spec,
+                pl.BlockSpec(
+                    (NPANEL, rows, TILE, TILE),
+                    lambda s, i, w: (0, jnp.where(s == 0, i, parts - 1), 0, 0),
+                ),
+            ),
+            scratch_shapes=[
+                pltpu.VMEM((NPANEL, PANEL, PANEL), jnp.bfloat16),
+                pltpu.VMEM((NPANEL, PANEL, PANEL), jnp.bfloat16),
+                pltpu.VMEM((PANEL, PANEL), jnp.bfloat16),
+                pltpu.VMEM((PANEL, PANEL), jnp.bfloat16),
+                pltpu.VMEM((rows * TILE, order), jnp.float32),
+            ],
+        ),
+        out_shape=(
+            factor_shape,
+            factor_shape,
+            jax.ShapeDtypeStruct((NPANEL, local_rows, TILE, TILE), jnp.float32),
+        ),
+        compiler_params=pltpu.CompilerParams(vmem_limit_bytes=48 * 2**20),
+        name="solve",
+    )(where, slabs, corner, inverses)
+
+    b_block = 4
+    row_spec = pl.BlockSpec((1, local_rows, TILE, order), lambda j, w, l: (0, 0, 0, 0))
+    col_spec = pl.BlockSpec((pl.Element(2), pl.Element(b_block // 2), pl.Element(TILE), pl.Element(order)),
+                            lambda j, w, l: (1, j * (b_block // 2), 0, 0))
+    front = pl.pallas_call(
+        functools.partial(update_kernel, local_cols),
+        grid_spec=pltpu.PrefetchScalarGridSpec(
+            num_scalar_prefetch=2,
+            grid=(local_cols // b_block,),
+            in_specs=[
+                row_spec, row_spec, col_spec, col_spec,
+                pl.BlockSpec((devices * CAP, TILE, TILE), lambda j, w, l: (0, 0, 0)),
+                pl.BlockSpec((NPANEL, local_rows, TILE, TILE), lambda j, w, l: (0, 0, 0, 0)),
+            ],
+            out_specs=pl.BlockSpec((local_rows, b_block, TILE, TILE), lambda j, w, l: (0, j, 0, 0)),
+        ),
+        out_shape=jax.ShapeDtypeStruct((local_rows, local_cols, TILE, TILE), jnp.float32),
+        compiler_params=pltpu.CompilerParams(vmem_limit_bytes=56 * 2**20),
+        name="update",
+    )(where, landing, high, low, high, low, arrived, own)
+    return front.reshape(local_rows, 1, local_cols, 1, TILE, TILE)
+
+
 def solution(mesh):
+    sizes = (mesh.shape["sib"], mesh.shape["row"], mesh.shape["col"])
     return jax.shard_map(
-        local,
+        local_fast if sizes == (2, 4, 4) else local,
         mesh=mesh,
         in_specs=(
             P("sib", ("row", "col"), None, None, None),

time: 790 us -> 569 us (0.72); the launches traced: 780 us -> 569 us
  Pallas kernels: 0 us -> 451 us
  waiting for transfers between devices: 475 us -> 89 us
  matrix products: 136 us -> 0 us
  local copies, waits for them, and re-layouts: 103 us -> 13.8 us
  other arithmetic: 39.1 us -> 2.4 us
  between operations: 14.6 us -> 0.94 us
    pallas_call x0 -> x4, Pallas kernels: none -> 451 us  [the longest x1 332 us: local_fast(): pl.pallas_call(exchange_kernel, out_shape=(jax.ShapeDtypeStruct((3, colum...]
    psum x2 -> x0, waiting for transfers between devices: 223 us -> none  [broadcast(): return lax.psum(kept, axis)]
    all_gather x2 -> x0, waiting for transfers between devices: 164 us -> none  [local(): everyone = lax.all_gather(column_block[None], 'col', axis=0, tiled=True)]
    dot_general x4 -> x0, matrix products: 136 us -> none  [the longest x2 119 us: local(): jnp.einsum('aip,bjp->abij', factor, column_factor, precision=lax.Precisio...]
    reshape x3 -> x1, local copies, waits for them, and re-layouts: 46.7 us -> 0.1 us  [local_fast(): landing = lax.all_to_all(destined.reshape(devices, CAP), axes, split_axis...]
    another operation x4 -> x1, other arithmetic: 18.1 us -> 0.08 us  [local_fast(): where = jnp.stack([my_row, my_col, my_col + 4, my_col]).astype(jnp.int32)]
    all_gather x2 -> x0, local copies, waits for them, and re-layouts: 13.9 us -> none  [local(): everyone = lax.all_gather(column_block[None], 'col', axis=0, tiled=True)]
    scatter-add x1 -> x0, other arithmetic: 13.9 us -> none  [local(): front_tiles.at[landing.reshape(-1)].add(arrived.reshape(-1, TILE, TILE))]
  transfers between devices with their start and end apart: 6 -> 2, of which waited for: 5 -> 1; matrix products, arithmetic and copies ran while one was open for 5% -> 2% of each run, Pallas kernels for 0% -> 0%
where the time goes in v1:
time: 569 us
  Pallas kernels  451 us (79%)
  waiting for transfers between devices  89 us (16%)
  local copies, waits for them, and re-layouts  13.8 us (2%)
  starting transfers between devices  12.3 us (2%)
    pallas_call x1, Pallas kernels, local_fast(): pl.pallas_call(exchange_kernel, out_shape=(jax.ShapeDtypeStruct((3, colum...  332 us
    all_to_all x1, waiting for transfers between devices, local_fast(): lax.all_to_all(outgoing.reshape(devices, CAP, TILE, TILE), axes, split_ax...  89 us
    pallas_call x1, Pallas kernels, local_fast(): pl.pallas_call(functools.partial(update_kernel, local_cols), grid_spec=pl...  77.2 us
    pallas_call x1, Pallas kernels, local_fast(): pl.pallas_call(solve_kernel, grid_spec=pltpu.PrefetchScalarGridSpec(num_s...  38 us
  transfers between devices with their start and end apart: 2, of which 1 were waited for; matrix products, arithmetic and copies ran while one was open for 2% of the time, Pallas kernels for 0%

profile of v1, /device:TPU:2, one launch (start us, length us, event | category | flops | bytes accessed | tf_op | source)
XLA Modules:
  0.0 568.9 jit_solution(8493109857984459499)
XLA Ops:
  0.0 0.0 copy-start.6
  0.8 0.7 and_select_fusion.7
  1.5 0.8 select_reduce_fusion
  2.3 0.2 convert_reduce_fusion
  2.6 0.7 scatter_custom_fusion
  3.2 0.7 all_to_all.9
  3.9 6.1 %all-to-all-start = ((s32[32,1,2]{2,1,0:T(1,128)}), s32[32,1,2]{2,1,0:T(1,128)S(1)}, u32[]{:S(2)}, u32[]{:S(2)}) async-start(s32[32,1,2]{2,1,0:T(1,128)} %bitcast.10), calls=%async_computation | async-start | bytes 32768 | tf_op jit(solution)/shard_map/all_to_all | solution.py:464
  10.1 2.5 broadcast_in_dim.41
  12.6 0.0 copy-done.6
  12.6 5.3 scatter_fusion
  17.9 0.0 all-to-all-done
  18.0 6.2 %all-to-all-start.1 = ((f32[32,2,128,128]{3,2,1,0:T(8,128)}), f32[32,2,128,128]{3,2,1,0:T(8,128)}, u32[]{:S(2)}, u32[]{:S(2)}) async-start(f32[32,2,128,128]{3,2,1,0:T(8,128)} %bitcast.51), calls=%async_computation.1 | async-start | bytes 8388608 | tf_op jit(solution)/shard_map/all_to_all | solution.py:461
  24.1 0.1 pad_add_fusion.where_ref
  24.2 0.0 copy-start.5
  24.2 0.5 broadcast.311
  24.7 0.6 reduce.3
  25.3 0.1 reshape.211.land_ref
  25.4 0.0 copy-start.4
  25.4 89.0 %all-to-all-done.1 = f32[32,2,128,128]{3,2,1,0:T(8,128)} async-done(((f32[32,2,128,128]{3,2,1,0:T(8,128)}), f32[32,2,128,128]{3,2,1,0:T(8,128)}, u32[]{:S(2)}, u32[]{:S(2)}) %all-to-all-start.1) | async-done | bytes 4194336 | tf_op jit(solution)/shard_map/all_to_all | solution.py:461
  114.4 0.0 copy-start.2
  114.4 3.6 collect.1.p_ref
  118.0 0.0 copy-start
  118.0 1.3 copy-done
  119.3 331.7 %exchange.1 = (f32[3,4,2,16,128,128]{5,4,3,2,1,0:T(8,128)}, f32[4,4,128,128]{3,2,1,0:T(8,128)}) custom-call(f32[2,16,128,128]{3,2,1,0:T(8,128)} %copy-done), custom_call_target="tpu_custom_call" | custom-call | tf_op jit(solution)/shard_map/exchange/pallas_call | solution.py:482
  451.1 0.0 copy-done.4
  451.1 0.0 copy-done.5
  451.1 0.0 copy-done.2
  451.1 0.0 copy-start.3
  451.1 1.2 copy-done.3
  452.4 38.0 %solve.1 = (bf16[3,16,128,1024]{3,2,1,0:T(8,128)(2,1)}, bf16[3,16,128,1024]{3,2,1,0:T(8,128)(2,1)}, f32[2,16,128,128]{3,2,1,0:T(8,128)S(1)}) custom-call(s32[4]{0:T(128)S(1)} %pad_add_fusion.where_ref, f32[3,4,2,16,128,128]{5,4,3,2,1,0:T(8,128)} %get-tuple-element.10.s_ref, f32[4,4,128,128]{3,2,1,0:T(8,128)S(1)} %copy-done.3, f32[2,512,512]{2,1,0:T(8,128)S(1)} %copy-done.2), custom_call_target="tpu_custom_call" | custom-call | tf_op jit(solution)/shard_map/solve/pallas_call | solution.py:507
  490.4 0.0 copy-start.1
  490.4 1.3 copy-done.1
  491.7 77.2 %update.1 = f32[16,32,128,128]{3,2,1,0:T(8,128)} custom-call(s32[4]{0:T(128)} %copy-done.5, s32[64]{0:T(128)} %copy-done.4, bf16[3,16,128,1024]{3,2,1,0:T(8,128)(2,1)} %get-tuple-element.12.rh_ref.ch_ref, bf16[3,16,128,1024]{3,2,1,0:T(8,128)(2,1)} %get-tuple-element.13.rl_ref.cl_ref, bf16[3,16,128,1024]{3,2,1,0:T(8,128)(2,1)} %get-tuple-element.12.rh_ref.ch_ref, ...), custom_call_target="tpu_custom_call" | custom-call | tf_op jit(solution)/shard_map/update/pallas_call | solution.py:546
  (3 shorter events, 0.0 us)
Async XLA Ops:
  0.0 12.6 %copy-start.6 = (f32[1,1,32,128,128]{4,3,2,1,0:T(8,128)S(1)}, f32[1,1,32,128,128]{4,3,2,1,0:T(8,128)}, u32[]{:S(2)}) copy-start(f32[1,1,32,128,128]{4,3,2,1,0:T(8,128)} %param.5) | copy-start | bytes 6291460
  3.9 14.0 %all-to-all-start = ((s32[32,1,2]{2,1,0:T(1,128)}), s32[32,1,2]{2,1,0:T(1,128)S(1)}, u32[]{:S(2)}, u32[]{:S(2)}) async-start(s32[32,1,2]{2,1,0:T(1,128)} %bitcast.10), calls=%async_computation | async-start | bytes 32768 | tf_op jit(solution)/shard_map/all_to_all | solution.py:464
  18.0 96.4 %all-to-all-start.1 = ((f32[32,2,128,128]{3,2,1,0:T(8,128)}), f32[32,2,128,128]{3,2,1,0:T(8,128)}, u32[]{:S(2)}, u32[]{:S(2)}) async-start(f32[32,2,128,128]{3,2,1,0:T(8,128)} %bitcast.51), calls=%async_computation.1 | async-start | bytes 8388608 | tf_op jit(solution)/shard_map/all_to_all | solution.py:461
  24.2 426.9 %copy-start.5 = (s32[4]{0:T(128)}, s32[4]{0:T(128)S(1)}, u32[]{:S(2)}) copy-start(s32[4]{0:T(128)S(1)} %pad_add_fusion.where_ref) | copy-start | bytes 52
  25.4 425.7 %copy-start.4 = (s32[64]{0:T(128)}, s32[64]{0:T(128)S(1)}, u32[]{:S(2)}) copy-start(s32[64]{0:T(128)S(1)} %reshape.211.land_ref) | copy-start | bytes 772
  114.4 336.7 %copy-start.2 = (f32[2,512,512]{2,1,0:T(8,128)S(1)}, f32[2,512,512]{2,1,0:T(8,128)}, u32[]{:S(2)}) copy-start(f32[2,512,512]{2,1,0:T(8,128)} %w_ref.1) | copy-start | bytes 6291460
  118.0 1.3 copy-start
  451.1 1.2 copy-start.3
  490.4 1.3 copy-start.1

commit v2 on v1

--- a/solution.py
+++ b/solution.py
@@ -159,9 +159,9 @@
 
 def exchange_kernel(
     p_ref, s_ref, z_ref,
-    own_sem, g_recv, up_send, down_send,
-    h_recv, x_send, y_send, core_send, copy_sem,
-    z_local, z_send, z_recv,
+    g_recv, up_send, down_send,
+    h_recv, x_send, y_send, core_send,
+    z_send, z_recv,
 ):
     x = lax.axis_index("sib")
     r = lax.axis_index("row")
@@ -203,9 +203,6 @@
     def down_copy(src, c, p):
         return remote(src, s_ref.at[0, c, p], down_send.at[c, p], g_recv.at[c, p], down)
 
-    def own_copy(p):
-        return pltpu.make_async_copy(p_ref.at[p], s_ref.at[0, z, p], own_sem.at[p])
-
     def plane_copies(src, c, p):
         there = s_ref.at[1 + x, c, p]
         recv = h_recv.at[x, c, p]
@@ -213,7 +210,6 @@
             remote(src, there, x_send.at[c, p], recv, x_peer),
             remote(src, there, y_send.at[c, p], recv, y_peer),
             remote(src, there, core_send.at[x, c, p], recv, core_peer),
-            pltpu.make_async_copy(src, there, copy_sem.at[c, p]),
         )
 
     def relay_x(c, p):
@@ -240,7 +236,6 @@
             def body(c=c, side=side):
                 if side == 0:
                     src = p_ref.at[p]
-                    own_copy(p).start()
                 else:
                     src = s_ref.at[0, c, p]
                     up_copy(src, c, p).wait_recv()
@@ -254,6 +249,9 @@
                     for copy in plane_copies(src, c, p):
                         copy.start()
 
+                if side == 0:
+                    s_ref[0, z, p] = p_ref[p]
+
             guarded(exists, body)
 
     def relay_step(p, t):
@@ -271,9 +269,6 @@
                     to_core(1 - x, c, p).start()
 
             guarded(exists, body)
-
-    def corner_local():
-        return pltpu.make_async_copy(s_ref.at[0, :, 0, 0], z_ref.at[r], z_local)
 
     def corner_x():
         return remote(s_ref.at[0, :, 0, 0], z_ref.at[r], z_send.at[0], z_recv.at[0], x_peer)
@@ -291,17 +286,11 @@
         if n:
             relay_step(*steps[n - 1])
         if n == 4:
-            own_copy(0).wait()
-
             @pl.when(x == 1)
             def _():
-                corner_local().start()
                 corner_x().start()
+                z_ref[r] = s_ref[0, :, 0, 0]
         if n == 5:
-            @pl.when(x == 1)
-            def _():
-                corner_local().wait()
-
             @pl.when(x == 0)
             def _():
                 corner_x().wait_recv()
@@ -312,7 +301,6 @@
             corner_y().start()
     relay_step(*steps[-1])
 
-    own_copy(1).wait()
     corner_y().wait_recv()
     pl.when(x == 1)(lambda: corner_x().wait_send())
     corner_core().wait_send()
@@ -328,11 +316,8 @@
 
                 @pl.when(is_source)
                 def _():
-                    first, second, third, here = plane_copies(src, c, p)
-                    first.wait_send()
-                    second.wait_send()
-                    third.wait_send()
-                    here.wait()
+                    for copy in plane_copies(src, c, p):
+                        copy.wait_send()
 
                 @pl.when(is_relay)
                 def _():
@@ -467,7 +452,6 @@
 
     vmem = pl.BlockSpec(memory_space=pltpu.VMEM)
     smem = pl.BlockSpec(memory_space=pltpu.SMEM)
-    anywhere = pl.BlockSpec(memory_space=pl.ANY)
     panels = pl.pallas_call(
         functools.partial(collect_kernel, local_cols),
         out_shape=jax.ShapeDtypeStruct((NPANEL, local_rows, TILE, TILE), jnp.float32),
@@ -485,20 +469,25 @@
             jax.ShapeDtypeStruct((3, columns, NPANEL, local_rows, TILE, TILE), jnp.float32),
             jax.ShapeDtypeStruct((4, columns, TILE, TILE), jnp.float32),
         ),
-        in_specs=[anywhere],
-        out_specs=(anywhere, anywhere),
+        in_specs=[vmem],
+        out_specs=(vmem, vmem),
         scratch_shapes=[
-            dma((NPANEL,)), dma(unit), dma(unit), dma(unit),
-            dma((2,) + unit), dma(unit), dma(unit), dma((2,) + unit), dma(unit),
-            dma, dma((3,)), dma((3,)),
+            dma(unit), dma(unit), dma(unit),
+            dma((2,) + unit), dma(unit), dma(unit), dma((2,) + unit),
+            dma((3,)), dma((3,)),
         ],
-        compiler_params=pltpu.CompilerParams(collective_id=0, has_side_effects=True),
+        compiler_params=pltpu.CompilerParams(
+            collective_id=0, has_side_effects=True, vmem_limit_bytes=40 * 2**20
+        ),
         name="exchange",
     )(panels)
 
     my_row = lax.axis_index(("sib", "row"))
     my_col = lax.axis_index("col")
-    where = jnp.stack([my_row, my_col, my_col + 4, my_col]).astype(jnp.int32)
+    my_sib = lax.axis_index("sib")
+    is_source = lax.axis_index("row") == my_col
+    picks = [jnp.where(is_source & (my_sib == k), 0, 1 + k) for k in range(2)]
+    where = jnp.stack([my_row, my_col, my_col + 4, my_col, 0 * my_col, *picks]).astype(jnp.int32)
     rows = 4
     order = NPANEL * PANEL
     factor_shape = jax.ShapeDtypeStruct((3, local_rows, TILE, order), jnp.bfloat16)
@@ -510,7 +499,7 @@
             num_scalar_prefetch=1,
             grid=(3, parts),
             in_specs=[
-                pl.BlockSpec((1, columns, NPANEL, rows, TILE, TILE), lambda s, i, w: (s, 0, 0, i, 0, 0)),
+                pl.BlockSpec((1, columns, NPANEL, rows, TILE, TILE), lambda s, i, w: (w[4 + s], 0, 0, i, 0, 0)),
                 pl.BlockSpec((4, columns, TILE, TILE), lambda s, i, w: (0, 0, 0, 0)),
                 pl.BlockSpec((NPANEL, PANEL, PANEL), lambda s, i, w: (0, 0, 0)),
             ],

time: 569 us -> 426 us (0.75)
  the two profiles are of different devices: /device:TPU:2 before, /device:TPU:5 now
where the time goes in v2:
time: 426 us
  Pallas kernels  308 us (72%)
  waiting for transfers between devices  90.3 us (21%)
  starting transfers between devices  12.6 us (3%)
  local copies, waits for them, and re-layouts  11.3 us (3%)
    pallas_call x1, Pallas kernels, local_fast(): pl.pallas_call(exchange_kernel, out_shape=(jax.ShapeDtypeStruct((3, colum...  189 us
    all_to_all x1, waiting for transfers between devices, local_fast(): lax.all_to_all(outgoing.reshape(devices, CAP, TILE, TILE), axes, split_ax...  90.3 us
    pallas_call x1, Pallas kernels, local_fast(): pl.pallas_call(functools.partial(update_kernel, local_cols), grid_spec=pl...  77.3 us
    pallas_call x1, Pallas kernels, local_fast(): pl.pallas_call(solve_kernel, grid_spec=pltpu.PrefetchScalarGridSpec(num_s...  38 us
  transfers between devices with their start and end apart: 2, of which 1 were waited for; matrix products, arithmetic and copies ran while one was open for 2% of the time, Pallas kernels for 0%

profile of v2, /device:TPU:5, one launch (start us, length us, event | category | flops | bytes accessed | tf_op | source)
XLA Modules:
  0.0 425.5 jit_solution(4243271318880170712)
XLA Ops:
  0.0 0.0 copy-start.4
  0.8 0.7 and_select_fusion.7
  1.5 0.8 select_reduce_fusion
  2.3 0.2 convert_reduce_fusion
  2.6 0.7 scatter_custom_fusion
  3.2 0.7 all_to_all.9
  3.9 6.4 %all-to-all-start = ((s32[32,1,2]{2,1,0:T(1,128)}), s32[32,1,2]{2,1,0:T(1,128)S(1)}, u32[]{:S(2)}, u32[]{:S(2)}) async-start(s32[32,1,2]{2,1,0:T(1,128)} %bitcast.12), calls=%async_computation | async-start | bytes 32768 | tf_op jit(solution)/shard_map/all_to_all | solution.py:449
  10.4 2.5 broadcast_in_dim.41
  12.9 0.0 copy-done.4
  12.9 5.3 %scatter_fusion = f32[64,128,128]{2,1,0:T(8,128)} fusion(f32[64,128,128]{2,1,0:T(8,128)} %broadcast_in_dim.41, s32[32]{0:T(128)S(1)} %fusion.7, f32[32,128,128]{2,1,0:T(8,128)S(1)} %bitcast.54), kind=kCustom, calls=%fused_computation.1 | custom fusion | bytes 6291584 | tf_op jit(solution)/shard_map/scatter | solution.py:443
  18.1 0.0 all-to-all-done
  18.1 6.2 %all-to-all-start.1 = ((f32[32,2,128,128]{3,2,1,0:T(8,128)}), f32[32,2,128,128]{3,2,1,0:T(8,128)}, u32[]{:S(2)}, u32[]{:S(2)}) async-start(f32[32,2,128,128]{3,2,1,0:T(8,128)} %bitcast.53), calls=%async_computation.1 | async-start | bytes 8388608 | tf_op jit(solution)/shard_map/all_to_all | solution.py:446
  24.3 0.1 stack.24.where_ref
  24.4 0.0 copy-start.3
  24.4 0.6 broadcast.311
  25.0 0.7 reduce.3
  25.8 0.1 reshape.211.land_ref
  25.9 0.0 copy-start.2
  25.9 90.3 %all-to-all-done.1 = f32[32,2,128,128]{3,2,1,0:T(8,128)} async-done(((f32[32,2,128,128]{3,2,1,0:T(8,128)}), f32[32,2,128,128]{3,2,1,0:T(8,128)}, u32[]{:S(2)}, u32[]{:S(2)}) %all-to-all-start.1) | async-done | bytes 4194336 | tf_op jit(solution)/shard_map/all_to_all | solution.py:446
  116.1 0.0 copy-start.1
  116.1 3.6 collect.1.p_ref
  119.8 189.1 %exchange.1 = (f32[3,4,2,16,128,128]{5,4,3,2,1,0:T(8,128)}, f32[4,4,128,128]{3,2,1,0:T(8,128)S(1)}) custom-call(f32[2,16,128,128]{3,2,1,0:T(8,128)S(1)} %collect.1.p_ref), custom_call_target="tpu_custom_call" | custom-call | tf_op jit(solution)/shard_map/exchange/pallas_call | solution.py:466
  308.8 0.0 copy-done.2
  308.8 0.0 copy-done.3
  308.9 0.0 copy-done.1
  308.9 38.0 %solve.1 = (bf16[3,16,128,1024]{3,2,1,0:T(8,128)(2,1)}, bf16[3,16,128,1024]{3,2,1,0:T(8,128)(2,1)}, f32[2,16,128,128]{3,2,1,0:T(8,128)S(1)}) custom-call(s32[7]{0:T(128)S(1)} %stack.24.where_ref, f32[3,4,2,16,128,128]{5,4,3,2,1,0:T(8,128)} %get-tuple-element.10.s_ref, f32[4,4,128,128]{3,2,1,0:T(8,128)S(1)} %get-tuple-element.11.z_ref, ...), custom_call_target="tpu_custom_call" | custom-call | tf_op jit(solution)/shard_map/solve/pallas_call | solution.py:496
  346.9 0.0 copy-start
  346.9 1.3 copy-done
  348.3 77.3 %update.1 = f32[16,32,128,128]{3,2,1,0:T(8,128)} custom-call(s32[7]{0:T(128)} %copy-done.3, s32[64]{0:T(128)} %copy-done.2, bf16[3,16,128,1024]{3,2,1,0:T(8,128)(2,1)} %get-tuple-element.12.rh_ref.ch_ref, bf16[3,16,128,1024]{3,2,1,0:T(8,128)(2,1)} %get-tuple-element.13.rl_ref.cl_ref, bf16[3,16,128,1024]{3,2,1,0:T(8,128)(2,1)} %get-tuple-element.12.rh_ref.ch_ref, ...), custom_call_target="tpu_custom_call" | custom-call | tf_op jit(solution)/shard_map/update/pallas_call | solution.py:535
  (3 shorter events, 0.0 us)
Async XLA Ops:
  0.0 12.9 %copy-start.4 = (f32[1,1,32,128,128]{4,3,2,1,0:T(8,128)S(1)}, f32[1,1,32,128,128]{4,3,2,1,0:T(8,128)}, u32[]{:S(2)}) copy-start(f32[1,1,32,128,128]{4,3,2,1,0:T(8,128)} %param.5) | copy-start | bytes 6291460
  3.9 14.2 %all-to-all-start = ((s32[32,1,2]{2,1,0:T(1,128)}), s32[32,1,2]{2,1,0:T(1,128)S(1)}, u32[]{:S(2)}, u32[]{:S(2)}) async-start(s32[32,1,2]{2,1,0:T(1,128)} %bitcast.12), calls=%async_computation | async-start | bytes 32768 | tf_op jit(solution)/shard_map/all_to_all | solution.py:449
  18.1 98.0 %all-to-all-start.1 = ((f32[32,2,128,128]{3,2,1,0:T(8,128)}), f32[32,2,128,128]{3,2,1,0:T(8,128)}, u32[]{:S(2)}, u32[]{:S(2)}) async-start(f32[32,2,128,128]{3,2,1,0:T(8,128)} %bitcast.53), calls=%async_computation.1 | async-start | bytes 8388608 | tf_op jit(solution)/shard_map/all_to_all | solution.py:446
  24.4 284.4 %copy-start.3 = (s32[7]{0:T(128)}, s32[7]{0:T(128)S(1)}, u32[]{:S(2)}) copy-start(s32[7]{0:T(128)S(1)} %stack.24.where_ref) | copy-start | bytes 88
  25.9 283.0 %copy-start.2 = (s32[64]{0:T(128)}, s32[64]{0:T(128)S(1)}, u32[]{:S(2)}) copy-start(s32[64]{0:T(128)S(1)} %reshape.211.land_ref) | copy-start | bytes 772
  116.1 192.7 %copy-start.1 = (f32[2,512,512]{2,1,0:T(8,128)S(1)}, f32[2,512,512]{2,1,0:T(8,128)}, u32[]{:S(2)}) copy-start(f32[2,512,512]{2,1,0:T(8,128)} %w_ref.1) | copy-start | bytes 6291460
  346.9 1.4 copy-start

commit v3 on v2

--- a/solution.py
+++ b/solution.py
@@ -347,85 +347,143 @@
     return dot(left[0], right[0]) + (dot(left[0], right[1]) + dot(left[1], right[0]))
 
 
-def solve_kernel(where_ref, s_ref, z_ref, w_ref, high_ref, low_ref, own_ref, wh, wl, qh, ql, full):
-    slab, part = pl.program_id(0), pl.program_id(1)
-    rows = s_ref.shape[3]
-
-    @pl.when((slab == 0) & (part == 0))
+def front_kernel(
+    local_cols, where_ref, land_ref, r_ref, c0_ref, c1_ref, z_ref, w_ref, tiles_ref, out_ref,
+    wh, wl, qh, ql, pend, lh, ll, prod, count, place, head, link,
+):
+    step = pl.program_id(0)
+    local_rows = out_ref.shape[0]
+    b_block = out_ref.shape[1]
+    group = 4
+
+    @pl.when(step == 0)
     def _():
         for p in range(NPANEL):
             wh[p], wl[p] = split(w_ref[p])
         corner = jnp.concatenate([z_ref[:, c].reshape(PANEL, TILE) for c in range(4)], axis=1)
         qh[...], ql[...] = split(dot3(split(corner), (wh[0], wl[0])))
-
-    def columns(p):
-        return jnp.concatenate(
-            [s_ref[0, c, p].reshape(rows * TILE, TILE) for c in range(4)], axis=1
-        )
-
-    a = part * rows + lax.broadcasted_iota(jnp.int32, (rows * TILE, 1), 0) // TILE
-    tile_row = a * 8 + where_ref[slab]
-    first = dot3(split(columns(0)), (wh[0], wl[0]))
-    first_parts = split(first)
-    rest = columns(1) - dot3(first_parts, (qh[...], ql[...]))
-    second = dot3(split(rest), (wh[1], wl[1]))
-    first = jnp.where(tile_row >= 4, first, 0.0)
-    second = jnp.where(tile_row >= 8, second, 0.0)
-    full[:, :PANEL] = first
-    full[:, PANEL:] = second
-    high, low = split(full[...])
-    high_ref[...] = high.reshape(high_ref.shape)
-    low_ref[...] = low.reshape(low_ref.shape)
-
-    @pl.when(slab == 0)
+        for n in range(5):
+            count[n] = 0
+
+        def clear(b, carry):
+            head[b] = -1
+            return carry
+
+        lax.fori_loop(0, local_cols, clear, 0)
+
+        def chain(n, carry):
+            spot = land_ref[n] - 1
+
+            @pl.when(spot >= 0)
+            def _():
+                b = lax.rem(spot, local_cols)
+                link[n] = head[b]
+                head[b] = n
+
+            return carry
+
+        lax.fori_loop(0, land_ref.shape[0], chain, 0)
+
+    def solve(kind, done):
+        base = jnp.where(kind == 0, 0, group + group * lax.rem(done, 2))
+        chunk = kind * (local_rows // group) + done
+        block = pend[pl.ds(base, group)].reshape(group * TILE, NPANEL * PANEL)
+        first = dot3(split(block[:, :PANEL]), (wh[0], wl[0]))
+        first_parts = split(first)
+        rest = block[:, PANEL:] - dot3(first_parts, (qh[...], ql[...]))
+        second = dot3(split(rest), (wh[1], wl[1]))
+        kept = []
+        for m in range(group):
+            spot = place[kind, done * group + m]
+            tile_row = jnp.where(kind == 0, spot * 8 + where_ref[0], spot * 4 + where_ref[1])
+            kept.append(jnp.where(tile_row >= 8, second[m * TILE : (m + 1) * TILE], 0.0))
+        second_parts = split(jnp.concatenate(kept, axis=0))
+        lh[chunk, :, :PANEL], ll[chunk, :, :PANEL] = first_parts
+        lh[chunk, :, PANEL:], ll[chunk, :, PANEL:] = second_parts
+
+    @pl.when(step < local_rows)
     def _():
-        for p in range(NPANEL):
-            start = pl.multiple_of(p * PANEL + where_ref[3] * TILE, TILE)
-            own_ref[p] = full[:, pl.ds(start, TILE)].reshape(rows, TILE, TILE)
-
-
-def update_kernel(local_cols, where_ref, land_ref, rh_ref, rl_ref, ch_ref, cl_ref, tiles_ref, own_ref, out_ref):
-    step = pl.program_id(0)
-    a_total, b_block = out_ref.shape[0], out_ref.shape[1]
-    pairs = b_block // 2
-    a_block = 4
-    depth = rh_ref.shape[-1]
-
-    def chunk(i, carry):
-        a0 = i * a_block
-        left = tuple(ref[0, pl.ds(a0, a_block)].reshape(a_block * TILE, depth) for ref in (rh_ref, rl_ref))
-        for k in range(2):
-            right = tuple(ref[k].reshape(pairs * TILE, depth) for ref in (ch_ref, cl_ref))
-            product = -dot3(left, right)
-            for m in range(pairs):
-                out_ref[pl.ds(a0, a_block), 2 * m + k] = product[:, m * TILE : (m + 1) * TILE].reshape(
-                    a_block, TILE, TILE
-                )
-        return carry
-
-    lax.fori_loop(0, a_total // a_block, chunk, 0)
-
-    def add(n, carry):
-        place = land_ref[n] - 1
-        b = lax.rem(place, local_cols) - step * b_block
-
-        @pl.when((place >= 0) & (b >= 0) & (b < b_block))
+        for kind, ref, slab in ((0, r_ref, 0), (1, c0_ref, 1), (1, c1_ref, 2)):
+            largest = jnp.max(jnp.abs(ref[...].reshape(-1, TILE)))
+
+            @pl.when((largest > 0) & (step * 8 + where_ref[slab] >= 4))
+            def _():
+                n = count[kind]
+                slot = lax.rem(n, group) if kind == 0 else group + lax.rem(n, 2 * group)
+                for p in range(NPANEL):
+                    for c in range(4):
+                        start = p * PANEL + c * TILE
+                        pend[slot, :, start : start + TILE] = ref[0, c, p, 0]
+                place[kind, n] = step if kind == 0 else 2 * step + slab - 1
+                count[kind] = n + 1
+
+        def flush(q, carry):
+            kind, partial = q // 2, lax.rem(q, 2)
+            n, done = count[kind], count[2 + kind]
+            full = n >= group * done + group
+            left_over = (step == local_rows - 1) & (n > group * done)
+
+            @pl.when(((partial == 0) & full) | ((partial == 1) & left_over))
+            def _():
+                solve(kind, done)
+                count[2 + kind] = done + 1
+
+            return carry
+
+        lax.fori_loop(0, 4, flush, 0)
+
+    @pl.when(step >= local_rows)
+    def _():
+        b0 = (step - local_rows) * b_block
+        live_rows = count[0]
+        out_ref[...] = jnp.zeros_like(out_ref)
+        for k in range(b_block):
+            n = count[4]
+
+            @pl.when((n < count[1]) & (place[1, n] == b0 + k))
+            def _():
+                @pl.when(lax.rem(n, group) == 0)
+                def _():
+                    column = local_rows // group + n // group
+
+                    def multiply(i, carry):
+                        prod[i] = -dot3((lh[i], ll[i]), (lh[column], ll[column]))
+                        return carry
+
+                    lax.fori_loop(0, count[2], multiply, 0)
+
+                lane = pl.multiple_of(lax.rem(n, group) * TILE, TILE)
+
+                def put(i, carry):
+                    row = pl.multiple_of(lax.rem(i, group) * TILE, TILE)
+                    out_ref[place[0, i], k] = prod[i // group, pl.ds(row, TILE), pl.ds(lane, TILE)]
+                    return carry
+
+                lax.fori_loop(0, live_rows, put, 0)
+                count[4] = n + 1
+
+            def add(n):
+                a = (land_ref[n] - 1) // local_cols
+                out_ref[a, k] = out_ref[a, k] + tiles_ref[n]
+                return link[n]
+
+            lax.while_loop(lambda n: n >= 0, add, head[b0 + k])
+
+        @pl.when(b0 == 0)
         def _():
-            a = place // local_cols
-            out_ref[a, b] = out_ref[a, b] + tiles_ref[n]
-
-        return carry
-
-    lax.fori_loop(0, land_ref.shape[0], add, 0)
-
-    @pl.when(step == 0)
-    def _():
-        for p in range(NPANEL):
-            @pl.when(where_ref[0] >= (p + 1) * 4)
-            def _():
-                out_ref[0, p] = own_ref[p, 0]
-
-            out_ref[1:, p] = own_ref[p, 1:]
+            def replace(i, carry):
+                a = place[0, i]
+                row = pl.multiple_of(lax.rem(i, group) * TILE, TILE)
+                for p in range(NPANEL):
+                    @pl.when(a * 8 + where_ref[0] >= (p + 1) * 4)
+                    def _():
+                        lane = pl.multiple_of(p * PANEL + where_ref[1] * TILE, TILE)
+                        at = (i // group, pl.ds(row, TILE), pl.ds(lane, TILE))
+                        out_ref[a, p] = lh[at].astype(jnp.float32) + ll[at].astype(jnp.float32)
+
+                return carry
+
+            lax.fori_loop(0, live_rows, replace, 0)
 
 
 def local_fast(child_tiles, child_rows, child_slots, tile_count, inverses):
@@ -488,66 +546,55 @@
     is_source = lax.axis_index("row") == my_col
     picks = [jnp.where(is_source & (my_sib == k), 0, 1 + k) for k in range(2)]
     where = jnp.stack([my_row, my_col, my_col + 4, my_col, 0 * my_col, *picks]).astype(jnp.int32)
-    rows = 4
+    b_block = 2
     order = NPANEL * PANEL
-    factor_shape = jax.ShapeDtypeStruct((3, local_rows, TILE, order), jnp.bfloat16)
-    factor_spec = pl.BlockSpec((1, rows, TILE, order), lambda s, i, w: (s, i, 0, 0))
-    parts = local_rows // rows
-    high, low, own = pl.pallas_call(
-        solve_kernel,
+    group = 4
+    scalar = pltpu.SMEM
+    last = local_rows - 1
+
+    def slab_spec(slab):
+        return pl.BlockSpec(
+            (1, columns, NPANEL, 1, TILE, TILE),
+            lambda j, w, l: (w[4 + slab], 0, 0, jnp.minimum(j, last), 0, 0),
+        )
+
+    def whole(*shape):
+        return pl.BlockSpec(shape, lambda j, w, l: (0,) * len(shape), pipeline_mode=pl.Buffered(1))
+
+    front = pl.pallas_call(
+        functools.partial(front_kernel, local_cols),
         grid_spec=pltpu.PrefetchScalarGridSpec(
-            num_scalar_prefetch=1,
-            grid=(3, parts),
+            num_scalar_prefetch=2,
+            grid=(local_rows + local_cols // b_block,),
             in_specs=[
-                pl.BlockSpec((1, columns, NPANEL, rows, TILE, TILE), lambda s, i, w: (w[4 + s], 0, 0, i, 0, 0)),
-                pl.BlockSpec((4, columns, TILE, TILE), lambda s, i, w: (0, 0, 0, 0)),
-                pl.BlockSpec((NPANEL, PANEL, PANEL), lambda s, i, w: (0, 0, 0)),
+                slab_spec(0), slab_spec(1), slab_spec(2),
+                whole(4, columns, TILE, TILE),
+                whole(NPANEL, PANEL, PANEL),
+                whole(devices * CAP, TILE, TILE),
             ],
-            out_specs=(
-                factor_spec,
-                factor_spec,
-                pl.BlockSpec(
-                    (NPANEL, rows, TILE, TILE),
-                    lambda s, i, w: (0, jnp.where(s == 0, i, parts - 1), 0, 0),
-                ),
+            out_specs=pl.BlockSpec(
+                (local_rows, b_block, TILE, TILE),
+                lambda j, w, l: (0, jnp.maximum(j - local_rows, 0), 0, 0),
             ),
             scratch_shapes=[
                 pltpu.VMEM((NPANEL, PANEL, PANEL), jnp.bfloat16),
                 pltpu.VMEM((NPANEL, PANEL, PANEL), jnp.bfloat16),
                 pltpu.VMEM((PANEL, PANEL), jnp.bfloat16),
                 pltpu.VMEM((PANEL, PANEL), jnp.bfloat16),
-                pltpu.VMEM((rows * TILE, order), jnp.float32),
+                pltpu.VMEM((3 * group, TILE, order), jnp.float32),
+                pltpu.VMEM(((local_rows + local_cols) // group, group * TILE, order), jnp.bfloat16),
+                pltpu.VMEM(((local_rows + local_cols) // group, group * TILE, order), jnp.bfloat16),
+                pltpu.VMEM((local_rows // group, group * TILE, group * TILE), jnp.float32),
+                scalar((8,), jnp.int32),
+                scalar((2, local_cols + group), jnp.int32),
+                scalar((local_cols,), jnp.int32),
+                scalar((devices * CAP,), jnp.int32),
             ],
         ),
-        out_shape=(
-            factor_shape,
-            factor_shape,
-            jax.ShapeDtypeStruct((NPANEL, local_rows, TILE, TILE), jnp.float32),
-        ),
-        compiler_params=pltpu.CompilerParams(vmem_limit_bytes=48 * 2**20),
-        name="solve",
-    )(where, slabs, corner, inverses)
-
-    b_block = 4
-    row_spec = pl.BlockSpec((1, local_rows, TILE, order), lambda j, w, l: (0, 0, 0, 0))
-    col_spec = pl.BlockSpec((pl.Element(2), pl.Element(b_block // 2), pl.Element(TILE), pl.Element(order)),
-                            lambda j, w, l: (1, j * (b_block // 2), 0, 0))
-    front = pl.pallas_call(
-        functools.partial(update_kernel, local_cols),
-        grid_spec=pltpu.PrefetchScalarGridSpec(
-            num_scalar_prefetch=2,
-            grid=(local_cols // b_block,),
-            in_specs=[
-                row_spec, row_spec, col_spec, col_spec,
-                pl.BlockSpec((devices * CAP, TILE, TILE), lambda j, w, l: (0, 0, 0)),
-                pl.BlockSpec((NPANEL, local_rows, TILE, TILE), lambda j, w, l: (0, 0, 0, 0)),
-            ],
-            out_specs=pl.BlockSpec((local_rows, b_block, TILE, TILE), lambda j, w, l: (0, j, 0, 0)),
-        ),
         out_shape=jax.ShapeDtypeStruct((local_rows, local_cols, TILE, TILE), jnp.float32),
-        compiler_params=pltpu.CompilerParams(vmem_limit_bytes=56 * 2**20),
-        name="update",
-    )(where, landing, high, low, high, low, arrived, own)
+        compiler_params=pltpu.CompilerParams(vmem_limit_bytes=62 * 2**20),
+        name="front",
+    )(where, landing, slabs, slabs, slabs, corner, inverses, arrived)
     return front.reshape(local_rows, 1, local_cols, 1, TILE, TILE)
 
 

time: 426 us -> 365 us (0.86)
  the two profiles are of different devices: /device:TPU:5 before, /device:TPU:26 now
where the time goes in v3:
time: 365 us; the launch traced here: 367 us
  Pallas kernels  252 us (69%)
  waiting for transfers between devices  88.3 us (24%)
  local copies, waits for them, and re-layouts  11.9 us (3%)
  starting transfers between devices  11.6 us (3%)
    pallas_call x1, Pallas kernels, local_fast(): pl.pallas_call(exchange_kernel, out_shape=(jax.ShapeDtypeStruct((3, colum...  188 us
    all_to_all x1, waiting for transfers between devices, local_fast(): lax.all_to_all(outgoing.reshape(devices, CAP, TILE, TILE), axes, split_ax...  88.3 us
    pallas_call x1, Pallas kernels, local_fast(): pl.pallas_call(functools.partial(front_kernel, local_cols), grid_spec=plt...  60.1 us
  transfers between devices with their start and end apart: 2, of which 1 were waited for; matrix products, arithmetic and copies ran while one was open for 3% of the time, Pallas kernels for 0%

profile of v3, /device:TPU:26, one launch (start us, length us, event | category | flops | bytes accessed | tf_op | source)
XLA Modules:
  0.0 366.8 jit_solution(13501932956042531247)
XLA Ops:
  0.0 0.0 copy-start.2
  0.8 0.7 and_select_fusion.7
  1.5 0.8 select_reduce_fusion
  2.3 0.2 convert_reduce_fusion
  2.6 0.7 scatter_custom_fusion
  3.2 0.7 all_to_all.9
  3.9 5.9 %all-to-all-start = ((s32[32,1,2]{2,1,0:T(1,128)}), s32[32,1,2]{2,1,0:T(1,128)S(1)}, u32[]{:S(2)}, u32[]{:S(2)}) async-start(s32[32,1,2]{2,1,0:T(1,128)} %bitcast.12), calls=%async_computation | async-start | bytes 32768 | tf_op jit(solution)/shard_map/all_to_all | solution.py:507
  9.8 2.5 broadcast_in_dim.41
  12.3 0.0 copy-done.2
  12.3 5.6 %scatter_fusion = f32[64,128,128]{2,1,0:T(8,128)} fusion(f32[64,128,128]{2,1,0:T(8,128)} %broadcast_in_dim.41, s32[32]{0:T(128)S(1)} %fusion.7, f32[32,128,128]{2,1,0:T(8,128)S(1)} %bitcast.54), kind=kCustom, calls=%fused_computation.1 | custom fusion | bytes 6291584 | tf_op jit(solution)/shard_map/scatter | solution.py:501
  17.9 0.0 all-to-all-done
  17.9 5.8 %all-to-all-start.1 = ((f32[32,2,128,128]{3,2,1,0:T(8,128)}), f32[32,2,128,128]{3,2,1,0:T(8,128)}, u32[]{:S(2)}, u32[]{:S(2)}) async-start(f32[32,2,128,128]{3,2,1,0:T(8,128)} %bitcast.53), calls=%async_computation.1 | async-start | bytes 8388608 | tf_op jit(solution)/shard_map/all_to_all | solution.py:504
  23.8 0.6 stack.24.where_ref
  24.4 0.6 broadcast.311
  25.0 0.7 reduce.3
  25.7 0.1 reshape.211.land_ref
  25.8 0.0 copy-start.1
  25.8 88.3 %all-to-all-done.1 = f32[32,2,128,128]{3,2,1,0:T(8,128)} async-done(((f32[32,2,128,128]{3,2,1,0:T(8,128)}), f32[32,2,128,128]{3,2,1,0:T(8,128)}, u32[]{:S(2)}, u32[]{:S(2)}) %all-to-all-start.1) | async-done | bytes 4194336 | tf_op jit(solution)/shard_map/all_to_all | solution.py:504
  114.1 3.5 collect.1.p_ref
  117.5 188.1 %exchange.1 = (f32[3,4,2,16,128,128]{5,4,3,2,1,0:T(8,128)}, f32[4,4,128,128]{3,2,1,0:T(8,128)S(1)}) custom-call(f32[2,16,128,128]{3,2,1,0:T(8,128)S(1)} %collect.1.p_ref), custom_call_target="tpu_custom_call" | custom-call | tf_op jit(solution)/shard_map/exchange/pallas_call | solution.py:524
  305.6 0.0 copy-done.1
  305.7 0.0 copy-start
  305.7 1.0 copy-done
  306.7 60.1 %front.1 = f32[16,32,128,128]{3,2,1,0:T(8,128)} custom-call(s32[7]{0:T(128)} %stack.24.where_ref, s32[64]{0:T(128)} %copy-done.1, f32[3,4,2,16,128,128]{5,4,3,2,1,0:T(8,128)} %get-tuple-element.7.r_ref.c0_ref.c1_ref, f32[3,4,2,16,128,128]{5,4,3,2,1,0:T(8,128)} %get-tuple-element.7.r_ref.c0_ref.c1_ref, ...), custom_call_target="tpu_custom_call" | custom-call | tf_op jit(solution)/shard_map/front/pallas_call | solution.py:564
  (3 shorter events, 0.0 us)
Async XLA Ops:
  0.0 12.3 %copy-start.2 = (f32[1,1,32,128,128]{4,3,2,1,0:T(8,128)S(1)}, f32[1,1,32,128,128]{4,3,2,1,0:T(8,128)}, u32[]{:S(2)}) copy-start(f32[1,1,32,128,128]{4,3,2,1,0:T(8,128)} %param.5) | copy-start | bytes 6291460
  3.9 14.0 %all-to-all-start = ((s32[32,1,2]{2,1,0:T(1,128)}), s32[32,1,2]{2,1,0:T(1,128)S(1)}, u32[]{:S(2)}, u32[]{:S(2)}) async-start(s32[32,1,2]{2,1,0:T(1,128)} %bitcast.12), calls=%async_computation | async-start | bytes 32768 | tf_op jit(solution)/shard_map/all_to_all | solution.py:507
  17.9 96.1 %all-to-all-start.1 = ((f32[32,2,128,128]{3,2,1,0:T(8,128)}), f32[32,2,128,128]{3,2,1,0:T(8,128)}, u32[]{:S(2)}, u32[]{:S(2)}) async-start(f32[32,2,128,128]{3,2,1,0:T(8,128)} %bitcast.53), calls=%async_computation.1 | async-start | bytes 8388608 | tf_op jit(solution)/shard_map/all_to_all | solution.py:504
  25.8 279.9 %copy-start.1 = (s32[64]{0:T(128)}, s32[64]{0:T(128)S(1)}, u32[]{:S(2)}) copy-start(s32[64]{0:T(128)S(1)} %reshape.211.land_ref) | copy-start | bytes 772
  305.7 1.0 copy-start

commit v4 on v3

--- a/solution.py
+++ b/solution.py
@@ -13,6 +13,7 @@
 NPANEL = 2
 CHILD_TILES = 64
 CAP = 2
+PACK = 11
 
 
 def broadcast(value, axis, source):
@@ -140,7 +141,7 @@
     return slot_place, target
 
 
-def collect_kernel(local_cols, land_ref, tiles_ref, out_ref):
+def collect_kernel(local_cols, land_ref, table_ref, tiles_ref, out_ref, pack_ref):
     out_ref[...] = jnp.zeros_like(out_ref)
 
     def step(n, carry):
@@ -155,6 +156,18 @@
         return carry
 
     lax.fori_loop(0, land_ref.shape[0], step, 0)
+    pack_ref[...] = jnp.zeros_like(pack_ref)
+
+    def pack(n, carry):
+        slot = table_ref[n]
+
+        @pl.when((slot >= 0) & (slot < PACK))
+        def _():
+            pack_ref[0, slot] = out_ref[lax.rem(n, NPANEL), n // NPANEL]
+
+        return carry
+
+    lax.fori_loop(0, table_ref.shape[0], pack, 0)
 
 
 def exchange_kernel(
@@ -280,26 +293,34 @@
         pair = z_ref.at[pl.ds(2 * y, 2)]
         return remote(pair, pair, z_send.at[2], z_recv.at[2], y_peer)
 
-    steps = [(p, t) for p in range(NPANEL) for t in range(4)]
+    def corner_first():
+        @pl.when(x == 1)
+        def _():
+            corner_x().start()
+            z_ref[r] = s_ref[0, :, 0, 0]
+
+    def corner_second():
+        @pl.when(x == 0)
+        def _():
+            corner_x().wait_recv()
+
+        corner_core().start()
+
+    def corner_third():
+        corner_core().wait_recv()
+        corner_y().start()
+
+    corner_steps = [corner_first, corner_second, corner_third]
+    steps = [(p, t) for p in range(p_ref.shape[0]) for t in range(4)]
     for n, (p, t) in enumerate(steps):
         gather_step(p, t)
+        if n >= 3 and corner_steps:
+            corner_steps.pop(0)()
         if n:
             relay_step(*steps[n - 1])
-        if n == 4:
-            @pl.when(x == 1)
-            def _():
-                corner_x().start()
-                z_ref[r] = s_ref[0, :, 0, 0]
-        if n == 5:
-            @pl.when(x == 0)
-            def _():
-                corner_x().wait_recv()
-
-            corner_core().start()
-        if n == 6:
-            corner_core().wait_recv()
-            corner_y().start()
     relay_step(*steps[-1])
+    for corner_step in corner_steps:
+        corner_step()
 
     corner_y().wait_recv()
     pl.when(x == 1)(lambda: corner_x().wait_send())
@@ -347,14 +368,17 @@
     return dot(left[0], right[0]) + (dot(left[0], right[1]) + dot(left[1], right[0]))
 
 
-def front_kernel(
-    local_cols, where_ref, land_ref, r_ref, c0_ref, c1_ref, z_ref, w_ref, tiles_ref, out_ref,
-    wh, wl, qh, ql, pend, lh, ll, prod, count, place, head, link,
-):
+def front_kernel(local_cols, packed, where_ref, land_ref, *refs):
+    if packed:
+        table_ref, packs_ref, *refs = refs
+    else:
+        r_ref, c0_ref, c1_ref, *refs = refs
+    z_ref, w_ref, tiles_ref, out_ref, wh, wl, qh, ql, pend, lh, ll, prod, count, place, head, link = refs
     step = pl.program_id(0)
     local_rows = out_ref.shape[0]
     b_block = out_ref.shape[1]
     group = 4
+    solve_steps = 1 if packed else local_rows
 
     @pl.when(step == 0)
     def _():
@@ -401,27 +425,41 @@
         lh[chunk, :, :PANEL], ll[chunk, :, :PANEL] = first_parts
         lh[chunk, :, PANEL:], ll[chunk, :, PANEL:] = second_parts
 
-    @pl.when(step < local_rows)
-    def _():
-        for kind, ref, slab in ((0, r_ref, 0), (1, c0_ref, 1), (1, c1_ref, 2)):
-            largest = jnp.max(jnp.abs(ref[...].reshape(-1, TILE)))
-
-            @pl.when((largest > 0) & (step * 8 + where_ref[slab] >= 4))
+    def take(a):
+        for kind, slab in ((0, 0), (1, 1), (1, 2)):
+            if packed:
+                spots = [
+                    [table_ref[((slab * 4 + c) * local_rows + a) * NPANEL + p] for c in range(4)]
+                    for p in range(NPANEL)
+                ]
+                largest = functools.reduce(jnp.maximum, spots[0] + spots[1])
+                is_live = largest >= 0
+            else:
+                ref = (r_ref, c0_ref, c1_ref)[slab]
+                is_live = jnp.max(jnp.abs(ref[...].reshape(-1, TILE))) > 0
+
+            @pl.when(is_live & (a * 8 + where_ref[slab] >= 4))
             def _():
                 n = count[kind]
                 slot = lax.rem(n, group) if kind == 0 else group + lax.rem(n, 2 * group)
                 for p in range(NPANEL):
                     for c in range(4):
                         start = p * PANEL + c * TILE
-                        pend[slot, :, start : start + TILE] = ref[0, c, p, 0]
-                place[kind, n] = step if kind == 0 else 2 * step + slab - 1
+                        if packed:
+                            spot = spots[p][c]
+                            tile = packs_ref[where_ref[4 + slab], c, 0, jnp.maximum(spot, 0)]
+                            tile = jnp.where(spot >= 0, tile, 0.0)
+                        else:
+                            tile = ref[0, c, p, 0]
+                        pend[slot, :, start : start + TILE] = tile
+                place[kind, n] = a if kind == 0 else 2 * a + slab - 1
                 count[kind] = n + 1
 
         def flush(q, carry):
             kind, partial = q // 2, lax.rem(q, 2)
             n, done = count[kind], count[2 + kind]
             full = n >= group * done + group
-            left_over = (step == local_rows - 1) & (n > group * done)
+            left_over = (a == local_rows - 1) & (n > group * done)
 
             @pl.when(((partial == 0) & full) | ((partial == 1) & left_over))
             def _():
@@ -432,9 +470,20 @@
 
         lax.fori_loop(0, 4, flush, 0)
 
-    @pl.when(step >= local_rows)
+    @pl.when(step < solve_steps)
     def _():
-        b0 = (step - local_rows) * b_block
+        if packed:
+            def take_one(a, carry):
+                take(a)
+                return carry
+
+            lax.fori_loop(0, local_rows, take_one, 0)
+        else:
+            take(step)
+
+    @pl.when(step >= solve_steps)
+    def _():
+        b0 = (step - solve_steps) * b_block
         live_rows = count[0]
         out_ref[...] = jnp.zeros_like(out_ref)
         for k in range(b_block):
@@ -510,46 +559,68 @@
 
     vmem = pl.BlockSpec(memory_space=pltpu.VMEM)
     smem = pl.BlockSpec(memory_space=pltpu.SMEM)
-    panels = pl.pallas_call(
+    spot = landing - 1
+    panel_spot = jnp.where(
+        (landing > 0) & (spot % local_cols < NPANEL),
+        spot // local_cols * NPANEL + spot % local_cols,
+        0,
+    )
+    all_places = jnp.arange(local_rows * NPANEL, dtype=jnp.int32)
+    is_live = jnp.any(panel_spot[None, :] == all_places[:, None], axis=1) | (all_places == 0)
+    earlier = is_live[None, :] & (all_places[None, :] < all_places[:, None])
+    table = jnp.where(is_live, jnp.sum(earlier.astype(jnp.int32), axis=1), -1)
+    tables = lax.all_gather(table, axes, axis=0, tiled=False)
+    fits = jnp.max(tables) < PACK
+
+    panels, pack = pl.pallas_call(
         functools.partial(collect_kernel, local_cols),
-        out_shape=jax.ShapeDtypeStruct((NPANEL, local_rows, TILE, TILE), jnp.float32),
-        in_specs=[smem, vmem],
-        out_specs=vmem,
+        out_shape=(
+            jax.ShapeDtypeStruct((NPANEL, local_rows, TILE, TILE), jnp.float32),
+            jax.ShapeDtypeStruct((1, PACK, TILE, TILE), jnp.float32),
+        ),
+        in_specs=[smem, smem, vmem],
+        out_specs=(vmem, vmem),
         compiler_params=pltpu.CompilerParams(vmem_limit_bytes=24 * 2**20),
         name="collect",
-    )(landing, arrived)
-
-    dma = pltpu.SemaphoreType.DMA
-    unit = (columns, NPANEL)
-    slabs, corner = pl.pallas_call(
-        exchange_kernel,
-        out_shape=(
-            jax.ShapeDtypeStruct((3, columns, NPANEL, local_rows, TILE, TILE), jnp.float32),
-            jax.ShapeDtypeStruct((4, columns, TILE, TILE), jnp.float32),
-        ),
-        in_specs=[vmem],
-        out_specs=(vmem, vmem),
-        scratch_shapes=[
-            dma(unit), dma(unit), dma(unit),
-            dma((2,) + unit), dma(unit), dma(unit), dma((2,) + unit),
-            dma((3,)), dma((3,)),
-        ],
-        compiler_params=pltpu.CompilerParams(
-            collective_id=0, has_side_effects=True, vmem_limit_bytes=40 * 2**20
-        ),
-        name="exchange",
-    )(panels)
-
+    )(landing, table, arrived)
+
+    my_sib = lax.axis_index("sib")
     my_row = lax.axis_index(("sib", "row"))
     my_col = lax.axis_index("col")
-    my_sib = lax.axis_index("sib")
     is_source = lax.axis_index("row") == my_col
     picks = [jnp.where(is_source & (my_sib == k), 0, 1 + k) for k in range(2)]
     where = jnp.stack([my_row, my_col, my_col + 4, my_col, 0 * my_col, *picks]).astype(jnp.int32)
+    by_grid_row = tables.reshape(grid_rows, columns * local_rows * NPANEL)
+    slab_tables = jnp.concatenate(
+        [lax.dynamic_index_in_dim(by_grid_row, g, 0, False) for g in (my_row, my_col, my_col + 4)]
+    )
+
+    dma = pltpu.SemaphoreType.DMA
+
+    def exchange(block, collective_id, name):
+        unit = (columns, block.shape[0])
+        return pl.pallas_call(
+            exchange_kernel,
+            out_shape=(
+                jax.ShapeDtypeStruct((3, columns, *block.shape), jnp.float32),
+                jax.ShapeDtypeStruct((4, columns, TILE, TILE), jnp.float32),
+            ),
+            in_specs=[vmem],
+            out_specs=(vmem, vmem),
+            scratch_shapes=[
+                dma(unit), dma(unit), dma(unit),
+                dma((2,) + unit), dma(unit), dma(unit), dma((2,) + unit),
+                dma((3,)), dma((3,)),
+            ],
+            compiler_params=pltpu.CompilerParams(
+                collective_id=collective_id, has_side_effects=True, vmem_limit_bytes=40 * 2**20
+            ),
+            name=name,
+        )(block)
+
     b_block = 2
     order = NPANEL * PANEL
     group = 4
-    scalar = pltpu.SMEM
     last = local_rows - 1
 
     def slab_spec(slab):
@@ -561,40 +632,53 @@
     def whole(*shape):
         return pl.BlockSpec(shape, lambda j, w, l: (0,) * len(shape), pipeline_mode=pl.Buffered(1))
 
-    front = pl.pallas_call(
-        functools.partial(front_kernel, local_cols),
-        grid_spec=pltpu.PrefetchScalarGridSpec(
-            num_scalar_prefetch=2,
-            grid=(local_rows + local_cols // b_block,),
-            in_specs=[
-                slab_spec(0), slab_spec(1), slab_spec(2),
-                whole(4, columns, TILE, TILE),
-                whole(NPANEL, PANEL, PANEL),
-                whole(devices * CAP, TILE, TILE),
-            ],
-            out_specs=pl.BlockSpec(
-                (local_rows, b_block, TILE, TILE),
-                lambda j, w, l: (0, jnp.maximum(j - local_rows, 0), 0, 0),
+    def finish(packed, slab_specs, slab_args, corner, name):
+        solve_steps = 1 if packed else local_rows
+        return pl.pallas_call(
+            functools.partial(front_kernel, local_cols, packed),
+            grid_spec=pltpu.PrefetchScalarGridSpec(
+                num_scalar_prefetch=2,
+                grid=(solve_steps + local_cols // b_block,),
+                in_specs=[
+                    *slab_specs,
+                    whole(4, columns, TILE, TILE),
+                    whole(NPANEL, PANEL, PANEL),
+                    whole(devices * CAP, TILE, TILE),
+                ],
+                out_specs=pl.BlockSpec(
+                    (local_rows, b_block, TILE, TILE),
+                    lambda j, w, l: (0, jnp.maximum(j - solve_steps, 0), 0, 0),
+                ),
+                scratch_shapes=[
+                    pltpu.VMEM((NPANEL, PANEL, PANEL), jnp.bfloat16),
+                    pltpu.VMEM((NPANEL, PANEL, PANEL), jnp.bfloat16),
+                    pltpu.VMEM((PANEL, PANEL), jnp.bfloat16),
+                    pltpu.VMEM((PANEL, PANEL), jnp.bfloat16),
+                    pltpu.VMEM((3 * group, TILE, order), jnp.float32),
+                    pltpu.VMEM(((local_rows + local_cols) // group, group * TILE, order), jnp.bfloat16),
+                    pltpu.VMEM(((local_rows + local_cols) // group, group * TILE, order), jnp.bfloat16),
+                    pltpu.VMEM((local_rows // group, group * TILE, group * TILE), jnp.float32),
+                    pltpu.SMEM((8,), jnp.int32),
+                    pltpu.SMEM((2, local_cols + group), jnp.int32),
+                    pltpu.SMEM((local_cols,), jnp.int32),
+                    pltpu.SMEM((devices * CAP,), jnp.int32),
+                ],
             ),
-            scratch_shapes=[
-                pltpu.VMEM((NPANEL, PANEL, PANEL), jnp.bfloat16),
-                pltpu.VMEM((NPANEL, PANEL, PANEL), jnp.bfloat16),
-                pltpu.VMEM((PANEL, PANEL), jnp.bfloat16),
-                pltpu.VMEM((PANEL, PANEL), jnp.bfloat16),
-                pltpu.VMEM((3 * group, TILE, order), jnp.float32),
-                pltpu.VMEM(((local_rows + local_cols) // group, group * TILE, order), jnp.bfloat16),
-                pltpu.VMEM(((local_rows + local_cols) // group, group * TILE, order), jnp.bfloat16),
-                pltpu.VMEM((local_rows // group, group * TILE, group * TILE), jnp.float32),
-                scalar((8,), jnp.int32),
-                scalar((2, local_cols + group), jnp.int32),
-                scalar((local_cols,), jnp.int32),
-                scalar((devices * CAP,), jnp.int32),
-            ],
-        ),
-        out_shape=jax.ShapeDtypeStruct((local_rows, local_cols, TILE, TILE), jnp.float32),
-        compiler_params=pltpu.CompilerParams(vmem_limit_bytes=62 * 2**20),
-        name="front",
-    )(where, landing, slabs, slabs, slabs, corner, inverses, arrived)
+            out_shape=jax.ShapeDtypeStruct((local_rows, local_cols, TILE, TILE), jnp.float32),
+            compiler_params=pltpu.CompilerParams(vmem_limit_bytes=62 * 2**20),
+            name=name,
+        )(where, landing, *slab_args, corner, inverses, arrived)
+
+    def by_packs():
+        packs, corner = exchange(pack, 1, "exchange_packs")
+        specs = [smem, whole(3, columns, 1, PACK, TILE, TILE)]
+        return finish(True, specs, [slab_tables, packs], corner, "front_packs")
+
+    def by_panels():
+        slabs, corner = exchange(panels, 0, "exchange_panels")
+        return finish(False, [slab_spec(k) for k in range(3)], [slabs] * 3, corner, "front_panels")
+
+    front = lax.cond(fits, by_packs, by_panels)
     return front.reshape(local_rows, 1, local_cols, 1, TILE, TILE)
 
 

time: 365 us -> 324 us (0.89)
  the two profiles are of different devices: /device:TPU:26 before, /device:TPU:2 now
where the time goes in v4:
time: 324 us; the launch traced here: 321 us
  blocking collectives  148 us (46%)
  Pallas kernels  140 us (43%)
  local copies, waits for them, and re-layouts  14.5 us (4%)
  starting transfers between devices  12 us (4%)
  other arithmetic  4.17 us (1%)
    all_gather x1, blocking collectives, local_fast(): tables = lax.all_gather(table, axes, axis=0, tiled=False)  148 us
    pallas_call x1, Pallas kernels, exchange(): pl.pallas_call(exchange_kernel, out_shape=(jax.ShapeDtypeStruct((3, colum...  85.7 us
    pallas_call x1, Pallas kernels, finish(): pl.pallas_call(functools.partial(front_kernel, local_cols, packed), grid_...  50.7 us
  transfers between devices with their start and end apart: 2, of which 0 were waited for; matrix products, arithmetic and copies ran while one was open for 3% of the time, Pallas kernels for 0%

profile of v4, /device:TPU:2, one launch (start us, length us, event | category | flops | bytes accessed | tf_op | source)
XLA Modules:
  0.0 321.0 jit_solution(11536553840630372800)
XLA Ops:
  0.0 0.0 copy-start.3
  0.8 0.7 and_select_fusion.10
  1.5 0.8 select_reduce_fusion
  2.3 0.2 convert_reduce_fusion.1
  2.6 0.7 scatter_custom_fusion
  3.2 0.7 all_to_all.9
  3.9 6.1 %all-to-all-start = ((s32[32,1,2]{2,1,0:T(1,128)}), s32[32,1,2]{2,1,0:T(1,128)S(1)}, u32[]{:S(2)}, u32[]{:S(2)}) async-start(s32[32,1,2]{2,1,0:T(1,128)} %bitcast.13), calls=%async_computation | async-start | bytes 32768 | tf_op jit(solution)/shard_map/all_to_all | solution.py:556
  10.1 2.5 broadcast_in_dim.48
  12.6 0.0 copy-done.3
  12.6 5.4 %scatter_fusion = f32[64,128,128]{2,1,0:T(8,128)} fusion(f32[64,128,128]{2,1,0:T(8,128)} %broadcast_in_dim.48, s32[32]{0:T(128)S(1)} %fusion.14, f32[32,128,128]{2,1,0:T(8,128)S(1)} %bitcast.77), kind=kCustom, calls=%fused_computation.1 | custom fusion | bytes 6291584 | tf_op jit(solution)/shard_map/scatter | solution.py:550
  18.0 0.0 all-to-all-done
  18.0 5.8 %all-to-all-start.1 = ((f32[32,2,128,128]{3,2,1,0:T(8,128)}), f32[32,2,128,128]{3,2,1,0:T(8,128)}, u32[]{:S(2)}, u32[]{:S(2)}) async-start(f32[32,2,128,128]{3,2,1,0:T(8,128)} %bitcast.76), calls=%async_computation.1 | async-start | bytes 8388608 | tf_op jit(solution)/shard_map/all_to_all | solution.py:553
  23.9 0.1 stack.24
  24.0 0.6 broadcast.426
  24.5 0.7 reduce.7
  25.3 0.1 reshape.284.land_ref
  25.4 0.1 fusion.2
  25.5 0.1 convert_reduce_fusion
  25.7 148.2 %all-gather = s32[32,1,32]{2,1,0:T(1,128)S(1)} all-gather(s32[1,1,32]{2,1,0:T(1,128)S(1)} %fusion.13), channel_id=1, replica_groups=mesh['sib'=2,'row'=4,'col'=4] {'sib','row','col'}, dimensions={0}, use_global_device_ids=true | all-gather | bytes 4224 | tf_op jit(solution)/shard_map/all_gather | solution.py:572
  173.9 1.4 fusion.17
  176.0 0.1 reshape.287
  176.1 0.0 all-to-all-done.1
  176.2 4.0 %collect.1 = (f32[2,16,128,128]{3,2,1,0:T(8,128)S(1)}, f32[1,11,128,128]{3,2,1,0:T(8,128)S(1)}) custom-call(s32[64]{0:T(128)S(1)} %reshape.284.land_ref, s32[32]{0:T(128)S(1)} %broadcast_select_fusion.table_ref, f32[64,128,128]{2,1,0:T(8,128)} %bitcast.19.tiles_ref), custom_call_target="tpu_custom_call" | custom-call | tf_op jit(solution)/shard_map/collect/pallas_call | solution.py:575
  180.2 140.8 %conditional.1 = (f32[16,1,32,1,128,128]{5,4,3,2,1,0:T(8,128)}) conditional(s32[]{:T(128)} %convert_element_type.11, (f32[2,16,128,128]{3,2,1,0:T(8,128)S(1)}, s32[7]{0:T(128)S(1)}, s32[64]{0:T(128)S(1)}, f32[2,512,512]{2,1,0:T(8,128)}, f32[64,128,128]{2,1,0:T(8,128)}) %tuple.13, (f32[1,11,128,128]{3,2,1,0:T(8,128)S(1)}, s32[7]{0:T(128)S(1)}, ...), branch_computations={%region_8.9_spmd, %region_9.10_spmd} | conditional | bytes 38797376 | solution.py:681
  180.2 85.7 %exchange_packs.1 = (f32[3,4,1,11,128,128]{5,4,3,2,1,0:T(8,128)S(1)}, f32[4,4,128,128]{3,2,1,0:T(8,128)S(1)}) custom-call(f32[1,11,128,128]{3,2,1,0:T(8,128)S(1)} %get-tuple-element.41.p_ref), custom_call_target="tpu_custom_call" | custom-call | tf_op jit(solution)/shard_map/cond/branch_1_fun/exchange_packs/pallas_call | solution.py:602
  265.9 0.0 copy-start
  265.9 3.3 %copy-done = f32[3,4,1,11,128,128]{5,4,3,2,1,0:T(8,128)} copy-done((f32[3,4,1,11,128,128]{5,4,3,2,1,0:T(8,128)}, f32[3,4,1,11,128,128]{5,4,3,2,1,0:T(8,128)S(1)}, u32[]{:S(2)}) %copy-start) | copy-done | bytes 8650776 | tf_op jit(solution)/shard_map/cond
  269.2 0.0 copy-start.2
  269.2 1.1 copy-done.2
  270.3 50.7 %front_packs.1 = f32[16,32,128,128]{3,2,1,0:T(8,128)} custom-call(s32[7]{0:T(128)S(1)} %get-tuple-element.38.where_ref, s32[64]{0:T(128)S(1)} %get-tuple-element.39.land_ref, s32[384]{0:T(512)S(1)} %get-tuple-element.40.refs_0_, f32[3,4,1,11,128,128]{5,4,3,2,1,0:T(8,128)} %copy-done, f32[4,4,128,128]{3,2,1,0:T(8,128)} %copy-done.2, ...), custom_call_target="tpu_custom_call" | custom-call | tf_op jit(solution)/shard_map/cond/branch_1_fun/front_packs/pallas_call | solution.py:637
  (9 shorter events, 0.1 us)
Async XLA Ops:
  0.0 12.6 %copy-start.3 = (f32[1,1,32,128,128]{4,3,2,1,0:T(8,128)S(1)}, f32[1,1,32,128,128]{4,3,2,1,0:T(8,128)}, u32[]{:S(2)}) copy-start(f32[1,1,32,128,128]{4,3,2,1,0:T(8,128)} %param.7) | copy-start | bytes 6291460
  3.9 14.1 %all-to-all-start = ((s32[32,1,2]{2,1,0:T(1,128)}), s32[32,1,2]{2,1,0:T(1,128)S(1)}, u32[]{:S(2)}, u32[]{:S(2)}) async-start(s32[32,1,2]{2,1,0:T(1,128)} %bitcast.13), calls=%async_computation | async-start | bytes 32768 | tf_op jit(solution)/shard_map/all_to_all | solution.py:556
  18.0 158.1 %all-to-all-start.1 = ((f32[32,2,128,128]{3,2,1,0:T(8,128)}), f32[32,2,128,128]{3,2,1,0:T(8,128)}, u32[]{:S(2)}, u32[]{:S(2)}) async-start(f32[32,2,128,128]{3,2,1,0:T(8,128)} %bitcast.76), calls=%async_computation.1 | async-start | bytes 8388608 | tf_op jit(solution)/shard_map/all_to_all | solution.py:553
  265.9 3.3 %copy-start = (f32[3,4,1,11,128,128]{5,4,3,2,1,0:T(8,128)}, f32[3,4,1,11,128,128]{5,4,3,2,1,0:T(8,128)S(1)}, u32[]{:S(2)}) copy-start(f32[3,4,1,11,128,128]{5,4,3,2,1,0:T(8,128)S(1)} %get-tuple-element.42.refs_1_) | copy-start | bytes 25952260 | tf_op jit(solution)/shard_map/cond
  269.2 1.1 copy-start.2
